TPU v7x, 128 devices: a whole 4x4x4 slice. The times are simulated.
128 devices in a mesh: tile: 32 (over y, z, core), shard: 4 (over x).
Axes of the slice: x: 4, y: 4, z: 4, core: 2. Of those that a mesh axis runs over, the one named last changes fastest.
Arguments:
- gaussians: float32 [59, 1048576], P(None, ('tile', 'shard')), may hold values from -10 to 10, as said below
- camera: float32 [4], replicated, may hold values from -1000 to 1000, as said below
- fetch_index: int32 [128, 8192], P(('tile', 'shard')), may hold values from 0 to 8191, as said below
- tile_ids: int32 [128, 16], P(('tile', 'shard')), may hold values from 0 to 2047, as said below
- tile_lists: int32 [128, 16, 1024], P(('tile', 'shard')), may hold values from 0 to 8191, as said below
- tile_counts: int32 [128, 16], P(('tile', 'shard')), may hold values from 1 to 1024, as said below
- tile_active: int32 [128, 16], P(('tile', 'shard')), may hold values 0 or 1
- target: float32 [3, 2048, 256], P(None, ('tile', 'shard')), may hold values from 0 to 1
Outputs:
- image: float32 [3, 2048, 256], P(None, ('tile', 'shard'))
- gaussian_grads: float32 [59, 1048576], P(None, ('tile', 'shard'))
Inputs may be any that keep to these rules, and one draw needn't show every extreme that they name: `fetch_index`: in row d, block s of 64 entries holds distinct indices into owner s's 8192 Gaussians; over all rows every Gaussian of every owner is named exactly once. `tile_ids`: each row is a part of one permutation of the 2048 screen tiles. `tile_lists`: on each device every table position 0 to 8191 appears once among the used entries of its tiles' lists, in order of increasing depth of the Gaussian; unused entries are 0. `tile_counts`: on each device the counts sum to 8192, and one tile has exactly 1024. `gaussians`: depth (row 2) lies between 2 and 8; the quaternion's w (row 6) lies between 1 and 2; each Gaussian projects near the tile that lists it. `camera`: fx and fy near 8 * 64; the principal point near the image centre.
All inputs are finite; a program needn't handle non-finite values. No bound on the sum of `tile_active` on one device may be relied on, other than what follows from the above.
Results may differ from a plain program's by a relative error of at most 0.0003.
Values sent between devices are 32-bit elements; how exact they have to be, the bound alone decides.
No kernel may reach another device: no remote copies, remote signals or barrier semaphores. Data moves between devices by JAX's collectives and lax.ppermute only.
A program may use at most 128 MiB of HBM per device.

v0:
```python
import jax
import jax.numpy as jnp
from jax import lax
from jax.sharding import PartitionSpec as P

TILE_SIDE = 16
SPAN = 256
TILES_X = 64


SH_ZERO = 0.28209479177387814
SH_ONE = 0.4886025119029199
SH_TWO = (
    1.0925484305920792,
    -1.0925484305920792,
    0.31539156525252005,
    -1.0925484305920792,
    0.5462742152960396,
)
SH_THREE = (
    -0.5900435899266435,
    2.890611442640554,
    -0.4570457994644658,
    0.3731763325901154,
    -0.4570457994644658,
    1.445305721320277,
    -0.5900435899266435,
)


def harmonics(dir_x, dir_y, dir_z):
    sq_x, sq_y, sq_z = (dir_x * dir_x, dir_y * dir_y, dir_z * dir_z)
    rows = [
        SH_ZERO * jnp.ones_like(dir_x),
        -SH_ONE * dir_y,
        SH_ONE * dir_z,
        -SH_ONE * dir_x,
        SH_TWO[0] * dir_x * dir_y,
        SH_TWO[1] * dir_y * dir_z,
        SH_TWO[2] * (2.0 * sq_z - sq_x - sq_y),
        SH_TWO[3] * dir_x * dir_z,
        SH_TWO[4] * (sq_x - sq_y),
        SH_THREE[0] * dir_y * (3.0 * sq_x - sq_y),
        SH_THREE[1] * dir_x * dir_y * dir_z,
        SH_THREE[2] * dir_y * (4.0 * sq_z - sq_x - sq_y),
        SH_THREE[3] * dir_z * (2.0 * sq_z - 3.0 * sq_x - 3.0 * sq_y),
        SH_THREE[4] * dir_x * (4.0 * sq_z - sq_x - sq_y),
        SH_THREE[5] * dir_z * (sq_x - sq_y),
        SH_THREE[6] * dir_x * (sq_x - 3.0 * sq_y),
    ]
    return jnp.stack(rows)


def project(table, camera):
    focal_x, focal_y, centre_x, centre_y = (camera[0], camera[1], camera[2], camera[3])
    mean_x, mean_y, mean_z = (table[0], table[1], table[2])
    spread = jnp.exp(table[3:6])
    quat = table[6:10]
    quat = quat / jnp.sqrt(jnp.sum(quat * quat, axis=0))
    w_part, x_part, y_part, z_part = (quat[0], quat[1], quat[2], quat[3])
    rotate = [
        [
            1.0 - 2.0 * (y_part * y_part + z_part * z_part),
            2.0 * (x_part * y_part - w_part * z_part),
            2.0 * (x_part * z_part + w_part * y_part),
        ],
        [
            2.0 * (x_part * y_part + w_part * z_part),
            1.0 - 2.0 * (x_part * x_part + z_part * z_part),
            2.0 * (y_part * z_part - w_part * x_part),
        ],
        [
            2.0 * (x_part * z_part - w_part * y_part),
            2.0 * (y_part * z_part + w_part * x_part),
            1.0 - 2.0 * (x_part * x_part + y_part * y_part),
        ],
    ]
    scaled = [[rotate[row][col] * spread[col] for col in range(3)] for row in range(3)]
    sigma = [
        [
            scaled[row][0] * scaled[col][0]
            + scaled[row][1] * scaled[col][1]
            + scaled[row][2] * scaled[col][2]
            for col in range(3)
        ]
        for row in range(3)
    ]
    depth_inv = 1.0 / mean_z
    zeros = jnp.zeros_like(mean_z)
    first_row = [focal_x * depth_inv, zeros, -focal_x * mean_x * depth_inv * depth_inv]
    second_row = [zeros, focal_y * depth_inv, -focal_y * mean_y * depth_inv * depth_inv]

    def quadric(left, right):
        total = zeros
        for row in range(3):
            for col in range(3):
                total = total + left[row] * sigma[row][col] * right[col]
        return total

    cov_a = quadric(first_row, first_row) + 0.3
    cov_b = quadric(first_row, second_row)
    cov_c = quadric(second_row, second_row) + 0.3
    determinant = cov_a * cov_c - cov_b * cov_b
    conic_a = cov_c / determinant
    conic_b = -cov_b / determinant
    conic_c = cov_a / determinant
    screen_x = focal_x * mean_x * depth_inv + centre_x
    screen_y = focal_y * mean_y * depth_inv + centre_y
    opacity = jax.nn.sigmoid(table[10])
    radius = jnp.sqrt(mean_x * mean_x + mean_y * mean_y + mean_z * mean_z)
    basis = harmonics(mean_x / radius, mean_y / radius, mean_z / radius)
    coeffs = table[11:59].reshape(3, 16, -1)
    colour = jnp.maximum(jnp.sum(coeffs * basis[None], axis=1) + 0.5, 0.0)
    return jnp.concatenate(
        [jnp.stack([screen_x, screen_y, conic_a, conic_b, conic_c, opacity]), colour], axis=0
    )


def tile_pass(features, tile, entries, count, live, goal):
    pixels = jnp.arange(TILE_SIDE * TILE_SIDE, dtype=jnp.int32)
    pixel_x = (tile % TILES_X * TILE_SIDE + pixels % TILE_SIDE).astype(jnp.float32) + 0.5
    pixel_y = (tile // TILES_X * TILE_SIDE + pixels // TILE_SIDE).astype(jnp.float32) + 0.5
    length = entries.shape[0]
    blocks = length // SPAN
    picked = features[:, entries].reshape(9, blocks, SPAN).transpose(1, 0, 2)
    keep = (
        ((jnp.arange(length, dtype=jnp.int32) < count) & (live > 0))
        .astype(jnp.float32)
        .reshape(blocks, SPAN)
    )

    @jax.checkpoint
    def advance(carry, block):
        transmit, colour = carry
        cols, kept = block
        delta_x = pixel_x[None, :] - cols[0][:, None]
        delta_y = pixel_y[None, :] - cols[1][:, None]
        power = (
            -0.5 * (cols[2][:, None] * delta_x * delta_x + cols[4][:, None] * delta_y * delta_y)
            - cols[3][:, None] * delta_x * delta_y
        )
        alphas = (cols[5] * kept)[:, None] * jnp.exp(power)
        logged = jnp.log1p(-alphas)
        running = jnp.cumsum(logged, axis=0)
        weights = alphas * transmit[None, :] * jnp.exp(running - logged)
        colour = colour + jnp.dot(cols[6:9], weights, precision=lax.Precision.HIGHEST)
        transmit = transmit * jnp.exp(running[-1])
        return ((transmit, colour), None)

    start = (
        jnp.ones((TILE_SIDE * TILE_SIDE,), jnp.float32),
        jnp.zeros((3, TILE_SIDE * TILE_SIDE), jnp.float32),
    )
    (transmit, colour), unused = lax.scan(advance, start, (picked, keep))
    residual = colour - goal
    loss = 0.5 * jnp.sum(residual * residual) * (live > 0).astype(jnp.float32)
    return (colour, loss)


def render_step(features, tiles, entries, counts, live, goal):

    def total(feats):

        def one_tile(pack):
            return tile_pass(feats, pack[0], pack[1], pack[2], pack[3], pack[4])

        colours, losses = lax.map(one_tile, (tiles, entries, counts, live, goal.transpose(1, 0, 2)))
        return (jnp.sum(losses), colours)

    loss, pullback, colours = jax.vjp(total, features, has_aux=True)
    grad_features = pullback(jnp.ones_like(loss))[0]
    return (colours.transpose(1, 0, 2), grad_features)


def per_device(
    gaussians, camera, fetch_index, tile_ids, tile_lists, tile_counts, tile_active, target
):
    wanted = fetch_index[0]
    asked = lax.all_to_all(wanted, ("tile", "shard"), split_axis=0, concat_axis=0, tiled=True)
    picked = gaussians[:, asked]

    def camera_map(values):
        return project(values, camera)

    table = lax.all_to_all(picked, ("tile", "shard"), split_axis=1, concat_axis=1, tiled=True)
    features, table_back = jax.vjp(camera_map, table)
    image, grad_features = render_step(
        features, tile_ids[0], tile_lists[0], tile_counts[0], tile_active[0], target
    )
    grad_table = table_back(grad_features)[0]
    returned = lax.all_to_all(
        grad_table, ("tile", "shard"), split_axis=1, concat_axis=1, tiled=True
    )
    grads = jnp.zeros_like(gaussians).at[:, asked].add(returned)
    return (image, grads)


def solution(mesh):
    in_specs = (
        P(None, ("tile", "shard")),
        P(),
        P(("tile", "shard"), None),
        P(("tile", "shard"), None),
        P(("tile", "shard"), None, None),
        P(("tile", "shard"), None),
        P(("tile", "shard"), None),
        P(None, ("tile", "shard"), None),
    )
    out_specs = (P(None, ("tile", "shard"), None), P(None, ("tile", "shard")))
    return jax.shard_map(
        per_device, mesh=mesh, in_specs=in_specs, out_specs=out_specs, check_vma=False
    )
```

profile of v0, /device:TPU:1, one launch (start us, length us, event | category | flops | bytes accessed | tf_op | source)
XLA Modules:
  0.0 1647.2 jit_solution(11193743795900233152)
XLA Ops:
  3.3 11.5 all-to-all-start
  26.2 29.9 %gather_fusion.1 = f32[8192,59]{1,0:T(8,128)} fusion(f32[59,8192]{0,1:T(8,128)} %copy.197, s32[8192]{0:T(1024)S(1)} %broadcast_clamp_fusion.1), kind=kCustom, calls=%fused_computation.1 | custom fusion | bytes 3899392 | tf_op jit(solution)/shard_map/gather | solution.py:180
  74.6 26.9 %all-to-all-done.1 = f32[128,1,3776]{2,1,0:T(1,128)S(1)} async-done(((f32[128,1,3776]{2,1,0:T(1,128)}), f32[128,1,3776]{2,1,0:T(1,128)S(1)}, u32[]{:S(2)}, u32[]{:S(2)}) %all-to-all-start.1) | async-done | bytes 1933344 | tf_op jit(solution)/shard_map/all_to_all | solution.py:185
  157.8 492.5 %while.116 = (s32[]{:T(128)}, f32[16,3,256]{2,0,1:T(8,128)}, s32[16,1024,1]{1,2,0:T(1,128)}, f32[16,256]{1,0:T(8,128)}, f32[16,256]{1,0:T(8,128)}, /*index=5*/f3...) while((s32[]{:T(128)}, f32[16,3,256]{2,0,1:T(8,128)}, ...), condition=%wide.region_7.8_spmd.clone, body=%wide.region_2.7_spmd.clone.sunk | while | flops 12667939 | bytes 2020410 | solution.py:167
  175.0 9.8 while.118
  205.8 9.8 while.118
  236.6 9.8 while.118
  267.4 9.8 while.118
  298.1 9.8 while.118
  328.9 9.8 while.118
  359.7 9.8 while.118
  390.5 9.8 while.118
  421.3 9.8 while.118
  452.1 9.8 while.118
  652.6 851.5 %while.114 = (s32[]{:T(128)}, f32[9,8192]{0,1:T(8,128)}, s32[16,1024,1]{1,2,0:T(1,128)}, f32[16,3,256]{2,1,0:T(4,128)}, f32[16]{0:T(128)}, /*index=5*/f32[16,4,2...) while((s32[]{:T(128)}, f32[9,8192]{0,1:T(8,128)}, ...), condition=%wide.region_23.24_spmd, body=%wide.region_8.23_spmd.sunk | while | flops 28993544 | bytes 7420432 | solution.py:167
  659.0 36.2 %while.117 = (s32[]{:T(128)}, f32[256]{0:T(256)S(1)}, f32[3,256]{1,0:T(4,128)}, f32[4,9,256]{2,1,0:T(8,128)S(1)}, f32[4,256]{1,0:T(4,128)S(1)}, /*index=5*/f32[4...) while((s32[]{:T(128)}, f32[256]{0:T(256)S(1)}, ...), condition=%wide.region_21.21_spmd.clone, body=%wide.region_9.20_spmd.clone.sunk | while | flops 28982788 | bytes 6779055 | solution.py:154
  695.5 11.4 scatter_fusion
  712.9 36.2 %while.117 = (s32[]{:T(128)}, f32[256]{0:T(256)S(1)}, f32[3,256]{1,0:T(4,128)}, f32[4,9,256]{2,1,0:T(8,128)S(1)}, f32[4,256]{1,0:T(4,128)S(1)}, /*index=5*/f32[4...) while((s32[]{:T(128)}, f32[256]{0:T(256)S(1)}, ...), condition=%wide.region_21.21_spmd.clone, body=%wide.region_9.20_spmd.clone.sunk | while | flops 28982788 | bytes 6779055 | solution.py:154
  749.4 10.1 scatter_fusion
  765.6 36.2 %while.117 = (s32[]{:T(128)}, f32[256]{0:T(256)S(1)}, f32[3,256]{1,0:T(4,128)}, f32[4,9,256]{2,1,0:T(8,128)S(1)}, f32[4,256]{1,0:T(4,128)S(1)}, /*index=5*/f32[4...) while((s32[]{:T(128)}, f32[256]{0:T(256)S(1)}, ...), condition=%wide.region_21.21_spmd.clone, body=%wide.region_9.20_spmd.clone.sunk | while | flops 28982788 | bytes 6779055 | solution.py:154
  802.0 10.5 scatter_fusion
  818.6 36.2 %while.117 = (s32[]{:T(128)}, f32[256]{0:T(256)S(1)}, f32[3,256]{1,0:T(4,128)}, f32[4,9,256]{2,1,0:T(8,128)S(1)}, f32[4,256]{1,0:T(4,128)S(1)}, /*index=5*/f32[4...) while((s32[]{:T(128)}, f32[256]{0:T(256)S(1)}, ...), condition=%wide.region_21.21_spmd.clone, body=%wide.region_9.20_spmd.clone.sunk | while | flops 28982788 | bytes 6779055 | solution.py:154
  855.1 10.5 scatter_fusion
  871.6 36.2 %while.117 = (s32[]{:T(128)}, f32[256]{0:T(256)S(1)}, f32[3,256]{1,0:T(4,128)}, f32[4,9,256]{2,1,0:T(8,128)S(1)}, f32[4,256]{1,0:T(4,128)S(1)}, /*index=5*/f32[4...) while((s32[]{:T(128)}, f32[256]{0:T(256)S(1)}, ...), condition=%wide.region_21.21_spmd.clone, body=%wide.region_9.20_spmd.clone.sunk | while | flops 28982788 | bytes 6779055 | solution.py:154
  908.1 10.9 scatter_fusion
  925.1 36.2 %while.117 = (s32[]{:T(128)}, f32[256]{0:T(256)S(1)}, f32[3,256]{1,0:T(4,128)}, f32[4,9,256]{2,1,0:T(8,128)S(1)}, f32[4,256]{1,0:T(4,128)S(1)}, /*index=5*/f32[4...) while((s32[]{:T(128)}, f32[256]{0:T(256)S(1)}, ...), condition=%wide.region_21.21_spmd.clone, body=%wide.region_9.20_spmd.clone.sunk | while | flops 28982788 | bytes 6779055 | solution.py:154
  961.5 10.1 scatter_fusion
  977.7 36.2 %while.117 = (s32[]{:T(128)}, f32[256]{0:T(256)S(1)}, f32[3,256]{1,0:T(4,128)}, f32[4,9,256]{2,1,0:T(8,128)S(1)}, f32[4,256]{1,0:T(4,128)S(1)}, /*index=5*/f32[4...) while((s32[]{:T(128)}, f32[256]{0:T(256)S(1)}, ...), condition=%wide.region_21.21_spmd.clone, body=%wide.region_9.20_spmd.clone.sunk | while | flops 28982788 | bytes 6779055 | solution.py:154
  1014.2 10.5 scatter_fusion
  1030.8 36.2 %while.117 = (s32[]{:T(128)}, f32[256]{0:T(256)S(1)}, f32[3,256]{1,0:T(4,128)}, f32[4,9,256]{2,1,0:T(8,128)S(1)}, f32[4,256]{1,0:T(4,128)S(1)}, /*index=5*/f32[4...) while((s32[]{:T(128)}, f32[256]{0:T(256)S(1)}, ...), condition=%wide.region_21.21_spmd.clone, body=%wide.region_9.20_spmd.clone.sunk | while | flops 28982788 | bytes 6779055 | solution.py:154
  1067.3 10.2 scatter_fusion
  1083.6 36.2 %while.117 = (s32[]{:T(128)}, f32[256]{0:T(256)S(1)}, f32[3,256]{1,0:T(4,128)}, f32[4,9,256]{2,1,0:T(8,128)S(1)}, f32[4,256]{1,0:T(4,128)S(1)}, /*index=5*/f32[4...) while((s32[]{:T(128)}, f32[256]{0:T(256)S(1)}, ...), condition=%wide.region_21.21_spmd.clone, body=%wide.region_9.20_spmd.clone.sunk | while | flops 28982788 | bytes 6779055 | solution.py:154
  1120.0 11.3 scatter_fusion
  1137.4 36.2 %while.117 = (s32[]{:T(128)}, f32[256]{0:T(256)S(1)}, f32[3,256]{1,0:T(4,128)}, f32[4,9,256]{2,1,0:T(8,128)S(1)}, f32[4,256]{1,0:T(4,128)S(1)}, /*index=5*/f32[4...) while((s32[]{:T(128)}, f32[256]{0:T(256)S(1)}, ...), condition=%wide.region_21.21_spmd.clone, body=%wide.region_9.20_spmd.clone.sunk | while | flops 28982788 | bytes 6779055 | solution.py:154
  1173.8 9.9 scatter_fusion
  1189.8 36.2 %while.117 = (s32[]{:T(128)}, f32[256]{0:T(256)S(1)}, f32[3,256]{1,0:T(4,128)}, f32[4,9,256]{2,1,0:T(8,128)S(1)}, f32[4,256]{1,0:T(4,128)S(1)}, /*index=5*/f32[4...) while((s32[]{:T(128)}, f32[256]{0:T(256)S(1)}, ...), condition=%wide.region_21.21_spmd.clone, body=%wide.region_9.20_spmd.clone.sunk | while | flops 28982788 | bytes 6779055 | solution.py:154
  1226.3 11.6 scatter_fusion
  1243.9 36.2 %while.117 = (s32[]{:T(128)}, f32[256]{0:T(256)S(1)}, f32[3,256]{1,0:T(4,128)}, f32[4,9,256]{2,1,0:T(8,128)S(1)}, f32[4,256]{1,0:T(4,128)S(1)}, /*index=5*/f32[4...) while((s32[]{:T(128)}, f32[256]{0:T(256)S(1)}, ...), condition=%wide.region_21.21_spmd.clone, body=%wide.region_9.20_spmd.clone.sunk | while | flops 28982788 | bytes 6779055 | solution.py:154
  1280.4 10.9 scatter_fusion
  1297.4 36.2 %while.117 = (s32[]{:T(128)}, f32[256]{0:T(256)S(1)}, f32[3,256]{1,0:T(4,128)}, f32[4,9,256]{2,1,0:T(8,128)S(1)}, f32[4,256]{1,0:T(4,128)S(1)}, /*index=5*/f32[4...) while((s32[]{:T(128)}, f32[256]{0:T(256)S(1)}, ...), condition=%wide.region_21.21_spmd.clone, body=%wide.region_9.20_spmd.clone.sunk | while | flops 28982788 | bytes 6779055 | solution.py:154
  1349.5 36.2 %while.117 = (s32[]{:T(128)}, f32[256]{0:T(256)S(1)}, f32[3,256]{1,0:T(4,128)}, f32[4,9,256]{2,1,0:T(8,128)S(1)}, f32[4,256]{1,0:T(4,128)S(1)}, /*index=5*/f32[4...) while((s32[]{:T(128)}, f32[256]{0:T(256)S(1)}, ...), condition=%wide.region_21.21_spmd.clone, body=%wide.region_9.20_spmd.clone.sunk | while | flops 28982788 | bytes 6779055 | solution.py:154
  1385.9 10.7 scatter_fusion
  1402.7 36.2 %while.117 = (s32[]{:T(128)}, f32[256]{0:T(256)S(1)}, f32[3,256]{1,0:T(4,128)}, f32[4,9,256]{2,1,0:T(8,128)S(1)}, f32[4,256]{1,0:T(4,128)S(1)}, /*index=5*/f32[4...) while((s32[]{:T(128)}, f32[256]{0:T(256)S(1)}, ...), condition=%wide.region_21.21_spmd.clone, body=%wide.region_9.20_spmd.clone.sunk | while | flops 28982788 | bytes 6779055 | solution.py:154
  1439.2 11.0 scatter_fusion
  1456.3 36.2 %while.117 = (s32[]{:T(128)}, f32[256]{0:T(256)S(1)}, f32[3,256]{1,0:T(4,128)}, f32[4,9,256]{2,1,0:T(8,128)S(1)}, f32[4,256]{1,0:T(4,128)S(1)}, /*index=5*/f32[4...) while((s32[]{:T(128)}, f32[256]{0:T(256)S(1)}, ...), condition=%wide.region_21.21_spmd.clone, body=%wide.region_9.20_spmd.clone.sunk | while | flops 28982788 | bytes 6779055 | solution.py:154
  1492.7 11.4 scatter_fusion
  1538.4 33.6 %all_to_all.33 = f32[128,1,3776]{2,1,0:T(1,128)S(1)} all-to-all(f32[128,1,3776]{2,1,0:T(1,128)} %reshape.1558), channel_id=1, replica_groups=mesh['tile'=32,'shard'=4] {'tile','shard'}, dimensions={0} | all-to-all | bytes 3866624 | tf_op jit(solution)/shard_map/all_to_all | solution.py:191
  1596.3 46.7 %scatter_custom_fusion.1 = f32[59,8192]{0,1:T(8,128)} fusion(s32[8192]{0:T(1024)} %bitcast.449, f32[8192,59]{1,0:T(8,128)} %copy.216, f32[]{:T(128)} %constant.333.clone.1), kind=kCustom, calls=%fused_computation.192 | custom fusion | flops 483328 | bytes 1933824 | tf_op jit(solution)/shard_map/scatter-add | solution.py:194
  (4466 shorter events, 1315.4 us)
Async XLA Ops:
  3.3 21.3 %all-to-all-start = ((s32[128,64,1]{1,2,0:T(1,128)}), s32[128,64,1]{1,2,0:T(1,128)S(1)}, u32[]{:S(2)}, u32[]{:S(2)}) async-start(s32[128,64,1]{1,2,0:T(1,128)} %bitcast.12), calls=%async_computation | async-start | bytes 131072 | tf_op jit(solution)/shard_map/all_to_all | solution.py:179
  67.6 4.4 copy-start.66
  67.6 6.3 copy-start.65
  67.6 33.8 %all-to-all-start.1 = ((f32[128,1,3776]{2,1,0:T(1,128)}), f32[128,1,3776]{2,1,0:T(1,128)S(1)}, u32[]{:S(2)}, u32[]{:S(2)}) async-start(f32[128,1,3776]{2,1,0:T(1,128)} %reshape.1556), calls=%async_computation.1 | async-start | bytes 3932160 | tf_op jit(solution)/shard_map/all_to_all | solution.py:185
  128.4 15.6 copy-start
  129.3 18.6 %copy-start.2 = (f32[1,8192]{1,0:T(1,128)}, f32[1,8192]{1,0:T(1,128)S(1)}, u32[]{:S(2)}) copy-start(f32[1,8192]{1,0:T(1,128)S(1)} %slice.223) | copy-start | bytes 98308
  139.6 4.3 copy-start.10
  139.6 4.3 copy-start.12
  139.6 4.3 copy-start.14
  147.9 3.9 copy-start.4
  147.9 4.0 copy-start.6
  147.9 5.6 copy-start.18
  147.9 5.6 copy-start.23
  148.0 5.6 copy-start.25
  148.0 5.6 copy-start.27
  1507.2 3.4 copy-start.1
  1507.3 3.4 copy-start.13
  1507.6 5.8 copy-start.56
  1507.6 6.2 copy-start.54
  1507.6 6.2 copy-start.55
  1507.6 7.6 copy-start.45
  1507.6 7.6 copy-start.9
  1509.0 6.4 copy-start.3
  1509.0 6.4 copy-start.5
  1509.0 6.4 copy-start.7
  1509.0 6.4 copy-start.11
  1509.0 6.4 copy-start.19
  1509.1 6.4 copy-start.29
  1509.1 6.4 copy-start.30
  1509.1 6.4 copy-start.31
  1509.1 6.4 copy-start.33
  1509.1 6.4 copy-start.35
  1509.1 6.4 copy-start.46
  1509.1 6.4 copy-start.47
  1509.1 6.4 copy-start.48
  1509.1 6.4 copy-start.49
  1509.1 6.4 copy-start.50
  1509.2 6.4 copy-start.51
  1509.2 6.4 copy-start.52
  1509.2 6.4 copy-start.53
  1513.4 7.6 copy-start.37
  1513.8 8.1 copy-start.44
  1513.8 8.2 copy-start.43
  1513.8 8.2 copy-start.42
  1513.8 8.2 copy-start.41
  1513.8 8.3 copy-start.40
  1513.8 8.3 copy-start.39
  1514.2 8.0 copy-start.16
  (24 other events, 56.3 us)
where the time goes:
time: 1670 us; the launch traced here: 1650 us
  other arithmetic  744 us (45%)
  local copies, waits for them, and re-layouts  487 us (29%)
  matrix products  253 us (15%)
  loops' own time  77.1 us (5%)
  blocking collectives  33.6 us (2%)
  waiting for transfers between devices  32.8 us (2%)
    another operation x599, other arithmetic  276 us
    dot_general x192, matrix products, advance(): jnp.dot(cols[6:9], weights, precision=lax.Precision.HIGHEST)  253 us
    scatter-add x16, other arithmetic, tile_pass(): picked = features[:, entries].reshape(9, blocks, SPAN).transpose(1, 0, 2)  171 us
    dynamic_update_slice x96, local copies, waits for them, and re-layouts, total(): lax.map(one_tile, (tiles, entries, counts, live, goal.transpose(1, 0, 2)))  83.3 us
    gather x16, local copies, waits for them, and re-layouts, tile_pass(): picked = features[:, entries].reshape(9, blocks, SPAN).transpose(1, 0, 2)  79.8 us
    dynamic_update_slice x48, other arithmetic, total(): lax.map(one_tile, (tiles, entries, counts, live, goal.transpose(1, 0, 2)))  62.5 us
    dynamic_slice x80, local copies, waits for them, and re-layouts, total(): lax.map(one_tile, (tiles, entries, counts, live, goal.transpose(1, 0, 2)))  62.5 us
    another operation x2, loops' own time, total(): lax.map(one_tile, (tiles, entries, counts, live, goal.transpose(1, 0, 2)))  56.8 us

commit v1 on v0

v1 whole, which is shorter than its diff:
```python
import functools

import jax
import jax.numpy as jnp
from jax import lax
from jax.experimental import pallas as pl
from jax.experimental.pallas import tpu as pltpu
from jax.sharding import PartitionSpec as P

AXES = ("tile", "shard")
SEG = 64
SEGS = 16
GROUP = SEG * SEGS
MAX_GROUPS = 9
STEPS = 16
LOG2E = 1.4426950408889634
LN2 = 0.6931471805599453
FEATS = 9
TRIPLE = (0, 1)
ROWS = 32 * (2 * FEATS + len(TRIPLE))
BACK_ROWS = 32 * 2 * FEATS

SH_ZERO = 0.28209479177387814
SH_ONE = 0.4886025119029199
SH_TWO = (
    1.0925484305920792,
    -1.0925484305920792,
    0.31539156525252005,
    -1.0925484305920792,
    0.5462742152960396,
)
SH_THREE = (
    -0.5900435899266435,
    2.890611442640554,
    -0.4570457994644658,
    0.3731763325901154,
    -0.4570457994644658,
    1.445305721320277,
    -0.5900435899266435,
)


def harmonics(dir_x, dir_y, dir_z):
    sq_x, sq_y, sq_z = (dir_x * dir_x, dir_y * dir_y, dir_z * dir_z)
    return [
        None,
        -SH_ONE * dir_y,
        SH_ONE * dir_z,
        -SH_ONE * dir_x,
        SH_TWO[0] * dir_x * dir_y,
        SH_TWO[1] * dir_y * dir_z,
        SH_TWO[2] * (2.0 * sq_z - sq_x - sq_y),
        SH_TWO[3] * dir_x * dir_z,
        SH_TWO[4] * (sq_x - sq_y),
        SH_THREE[0] * dir_y * (3.0 * sq_x - sq_y),
        SH_THREE[1] * dir_x * dir_y * dir_z,
        SH_THREE[2] * dir_y * (4.0 * sq_z - sq_x - sq_y),
        SH_THREE[3] * dir_z * (2.0 * sq_z - 3.0 * sq_x - 3.0 * sq_y),
        SH_THREE[4] * dir_x * (4.0 * sq_z - sq_x - sq_y),
        SH_THREE[5] * dir_z * (sq_x - sq_y),
        SH_THREE[6] * dir_x * (sq_x - 3.0 * sq_y),
    ]


def project(rows, camera):
    focal_x, focal_y, centre_x, centre_y = camera
    mean_x, mean_y, mean_z = rows[0:3]
    spread = [jnp.exp(row) for row in rows[3:6]]
    q_w, q_x, q_y, q_z = rows[6:10]
    scale = lax.rsqrt(q_w * q_w + q_x * q_x + q_y * q_y + q_z * q_z)
    w_part, x_part, y_part, z_part = (q_w * scale, q_x * scale, q_y * scale, q_z * scale)
    rotate = [
        [
            1.0 - 2.0 * (y_part * y_part + z_part * z_part),
            2.0 * (x_part * y_part - w_part * z_part),
            2.0 * (x_part * z_part + w_part * y_part),
        ],
        [
            2.0 * (x_part * y_part + w_part * z_part),
            1.0 - 2.0 * (x_part * x_part + z_part * z_part),
            2.0 * (y_part * z_part - w_part * x_part),
        ],
        [
            2.0 * (x_part * z_part - w_part * y_part),
            2.0 * (y_part * z_part + w_part * x_part),
            1.0 - 2.0 * (x_part * x_part + y_part * y_part),
        ],
    ]
    depth_inv = 1.0 / mean_z
    along_x = mean_x * depth_inv
    along_y = mean_y * depth_inv
    lens_x = focal_x * depth_inv
    lens_y = focal_y * depth_inv
    first = [lens_x * (rotate[0][c] - along_x * rotate[2][c]) * spread[c] for c in range(3)]
    second = [lens_y * (rotate[1][c] - along_y * rotate[2][c]) * spread[c] for c in range(3)]
    cov_a = first[0] * first[0] + first[1] * first[1] + first[2] * first[2] + 0.3
    cov_b = first[0] * second[0] + first[1] * second[1] + first[2] * second[2]
    cov_c = second[0] * second[0] + second[1] * second[1] + second[2] * second[2] + 0.3
    inverse = LOG2E / (cov_a * cov_c - cov_b * cov_b)
    conic_a = -0.5 * cov_c * inverse
    conic_b = cov_b * inverse
    conic_c = -0.5 * cov_a * inverse
    screen_x = focal_x * along_x + centre_x
    screen_y = focal_y * along_y + centre_y
    opacity = -LOG2E * jnp.log(1.0 + jnp.exp(-rows[10]))
    radius = lax.rsqrt(mean_x * mean_x + mean_y * mean_y + mean_z * mean_z)
    basis = harmonics(mean_x * radius, mean_y * radius, mean_z * radius)
    colours = []
    for k in range(3):
        total = SH_ZERO * rows[11 + 16 * k] + 0.5
        for j in range(1, 16):
            total = total + basis[j] * rows[11 + 16 * k + j]
        colours.append(jnp.maximum(total, 0.0))
    return [screen_x, screen_y, conic_a, conic_b, conic_c, opacity] + colours


def low_half(shape):
    return lax.broadcasted_iota(jnp.int32, shape, len(shape) - 1) < 64


def swap(values):
    return pltpu.roll(values, 64, axis=1)


def spread_tiles(gaussians_ref, flat_ref):
    def body(t, carry):
        lanes = pl.ds(pl.multiple_of(t * 128, 128), 128)
        for g in range(8):
            size = 8 if g < 7 else 3
            start = pl.multiple_of((g * 64 + t) * 8, 8)
            flat_ref[pl.ds(start, size), :] = gaussians_ref[8 * g : 8 * g + size, lanes]
        return carry

    lax.fori_loop(0, 64, body, 0, unroll=4)


def param_rows(flat_ref, chunk, size):
    return [
        flat_ref[pl.ds((k // 8) * 512 + k % 8 + chunk * size * 8, size, stride=8), :]
        for k in range(59)
    ]


def parts(values, count):
    out = []
    for step in range(count):
        piece = values.astype(jnp.bfloat16)
        out.append(piece)
        if step + 1 < count:
            values = values - piece.astype(jnp.float32)
    return out


def pack_table(table_ref, packed_ref):
    extra = 2 * FEATS
    for f in range(FEATS):
        whole = jnp.concatenate(
            [table_ref[f, pl.ds(0, 32, stride=2), :], table_ref[f, pl.ds(1, 32, stride=2), :]], axis=1
        )
        pieces = parts(whole, 3 if f in TRIPLE else 2)
        packed_ref[64 * f : 64 * f + 32, :] = pieces[0]
        packed_ref[64 * f + 32 : 64 * f + 64, :] = pieces[1]
        if f in TRIPLE:
            packed_ref[32 * extra : 32 * extra + 32, :] = pieces[2]
            extra += 1


def one_hot(index):
    count = index.shape[1]
    rows = lax.broadcasted_iota(jnp.int32, (256, count), 0)
    return jnp.where(rows == (index & 255), 1.0, 0.0).astype(jnp.bfloat16)


def upper_mask(index):
    count = index.shape[1]
    rows = lax.broadcasted_iota(jnp.int32, (32, count), 0)
    return jnp.where(rows == (index >> 8), 1.0, 0.0)


def gather_features(packed_ref, index):
    mask = upper_mask(index)
    found = jnp.dot(packed_ref[...], one_hot(index), preferred_element_type=jnp.float32)
    out = []
    extra = 2 * FEATS
    for f in range(FEATS):
        block = found[64 * f : 64 * f + 32] + found[64 * f + 32 : 64 * f + 64]
        if f in TRIPLE:
            block = block + found[32 * extra : 32 * extra + 32]
            extra += 1
        out.append(jnp.sum(block * mask, axis=0, keepdims=True))
    return out


def one_hot_rows(column):
    lanes = lax.broadcasted_iota(jnp.int32, (column.shape[0], 256), 1)
    return jnp.where(lanes == (column.astype(jnp.int32) & 255), 1.0, 0.0).astype(jnp.bfloat16)


def scatter_features(total_ref, rows, index, column):
    mask = upper_mask(index).astype(jnp.bfloat16)
    blocks = []
    for row in rows:
        for piece in parts(row, 2):
            blocks.append(mask * piece)
    total_ref[...] += jnp.dot(
        jnp.concatenate(blocks, axis=0), one_hot_rows(column), preferred_element_type=jnp.float32
    )


def unpack_total(total_ref, table_ref):
    for f in range(FEATS):
        whole = total_ref[64 * f : 64 * f + 32, :] + total_ref[64 * f + 32 : 64 * f + 64, :]
        table_ref[f, pl.ds(0, 32, stride=2), :] = whole[:, :128]
        table_ref[f, pl.ds(1, 32, stride=2), :] = whole[:, 128:]


def table_to_blocks(table_ref, out_ref):
    low = low_half((64, 128))
    for i in range(5):
        even = table_ref[2 * i]
        odd = table_ref[2 * i + 1] if 2 * i + 1 < FEATS else jnp.zeros((64, 128), jnp.float32)
        out_ref[pl.ds(i, 64, stride=10), :] = jnp.where(low, even, swap(odd))
        out_ref[pl.ds(5 + i, 64, stride=10), :] = jnp.where(low, swap(even), odd)


def blocks_to_table(in_ref, table_ref):
    low = low_half((64, 128))
    for i in range(5):
        first = in_ref[pl.ds(i, 64, stride=10), :]
        second = in_ref[pl.ds(5 + i, 64, stride=10), :]
        table_ref[2 * i] = jnp.where(low, first, swap(second))
        if 2 * i + 1 < FEATS:
            table_ref[2 * i + 1] = jnp.where(low, swap(first), second)


def row_of(ref, q):
    return jnp.concatenate([ref[pl.ds(4 * q + c, 1), :] for c in range(4)], axis=1)


CHUNK = 8


def project_kernel(camera_ref, gaussians_ref, packed_ref, flat_ref, table_ref):
    camera = [camera_ref[k] for k in range(4)]
    spread_tiles(gaussians_ref, flat_ref)

    def body(chunk, carry):
        features = project(param_rows(flat_ref, chunk, CHUNK), camera)
        for f in range(FEATS):
            table_ref[f, pl.ds(pl.multiple_of(chunk * CHUNK, CHUNK), CHUNK), :] = features[f]
        return carry

    lax.fori_loop(0, 64 // CHUNK, body, 0)
    pack_table(table_ref, packed_ref)


def fetch_kernel(parity_ref, packed_ref, asked_ref, index_ref, send_ref, table_ref):
    low = low_half((64, 128))
    even = asked_ref[pl.ds(0, 64, stride=2), :]
    odd = asked_ref[pl.ds(1, 64, stride=2), :]
    index_ref[...] = jnp.where(
        parity_ref[0] == 0,
        jnp.where(low, even, swap(odd)),
        jnp.where(low, swap(even), odd),
    )

    def body(q, carry):
        rows = gather_features(packed_ref, row_of(index_ref, q))
        for f in range(FEATS):
            for c in range(4):
                table_ref[f, pl.ds(4 * q + c, 1), :] = rows[f][:, 128 * c : 128 * c + 128]
        return carry

    lax.fori_loop(0, 16, body, 0)
    table_to_blocks(table_ref, send_ref)


def return_kernel(camera_ref, gaussians_ref, index_ref, back_ref, grads_ref, flat_ref, table_ref, total_ref):
    camera = [camera_ref[k] for k in range(4)]
    spread_tiles(gaussians_ref, flat_ref)
    blocks_to_table(back_ref, table_ref)
    total_ref[...] = jnp.zeros_like(total_ref)
    columns = jnp.concatenate([index_ref[...].astype(jnp.float32), jnp.zeros((64, 128), jnp.float32)], axis=0).T
    for q in range(16):
        rows = [row_of(table_ref.at[f], q) for f in range(FEATS)]
        column = jnp.concatenate([columns[:, 4 * q + c : 4 * q + c + 1] for c in range(4)], axis=0)
        scatter_features(total_ref, rows, row_of(index_ref, q), column)
    unpack_total(total_ref, table_ref)

    def body(chunk, carry):
        params = param_rows(flat_ref, chunk, CHUNK)
        _, pullback = jax.vjp(lambda rows: project(rows, camera), params)
        place = pl.ds(pl.multiple_of(chunk * CHUNK, CHUNK), CHUNK)
        (grads,) = pullback([table_ref[f, place, :] for f in range(FEATS)])
        for k in range(59):
            start = (k // 8) * 512 + k % 8 + chunk * CHUNK * 8
            flat_ref[pl.ds(start, CHUNK, stride=8), :] = grads[k]
        return carry

    lax.fori_loop(0, 64 // CHUNK, body, 0)

    def out(t, carry):
        lanes = pl.ds(pl.multiple_of(t * 128, 128), 128)
        for g in range(8):
            size = 8 if g < 7 else 3
            start = pl.multiple_of((g * 64 + t) * 8, 8)
            grads_ref[8 * g : 8 * g + size, lanes] = flat_ref[pl.ds(start, size), :]
        return carry

    lax.fori_loop(0, 64, out, 0, unroll=4)


def monomials():
    lane = lax.broadcasted_iota(jnp.int32, (1, 256), 1)
    x = (lane & 15).astype(jnp.float32) - 7.5
    y = (lane >> 4).astype(jnp.float32) - 7.5
    return [jnp.ones((1, 256), jnp.float32), x, y, x * x, x * y, y * y]


def render_kernel(
    ids_ref,
    counts_ref,
    active_ref,
    recv_ref,
    lists_ref,
    target_ref,
    image_ref,
    send_ref,
    seg_tile,
    seg_place,
    table_ref,
    packed_ref,
    total_ref,
    basis_ref,
    moment_ref,
    index_ref,
    shape_ref,
    coef_ref,
    wide_ref,
    power_ref,
    alpha_ref,
    weight_ref,
    pass_ref,
    light_ref,
    start_ref,
    behind_ref,
    resid_ref,
    resid_rows_ref,
    pieces_ref,
    sums_ref,
):
    def clear(n, carry):
        seg_tile[n] = 0
        seg_place[n] = 16
        return carry

    lax.fori_loop(0, SEGS * MAX_GROUPS, clear, 0)

    def add_tile(t, n):
        used = jnp.where(active_ref[0, t] > 0, (counts_ref[0, t] + (SEG - 1)) >> 6, 0)

        def add_segment(k, m):
            seg_tile[m] = t
            seg_place[m] = k
            return m + 1

        return lax.fori_loop(0, used, add_segment, n)

    segments = lax.fori_loop(0, 16, add_tile, 0)
    groups = (segments + (SEGS - 1)) // SEGS

    blocks_to_table(recv_ref, table_ref)
    pack_table(table_ref, packed_ref)
    total_ref[...] = jnp.zeros_like(total_ref)
    pass_ref[...] = jnp.ones_like(pass_ref)
    light_ref[...] = jnp.zeros_like(light_ref)
    coef_ref[...] = jnp.zeros_like(coef_ref)
    start_ref[256:272, :] = jnp.zeros((16, 256), jnp.float32)
    behind_ref[256:272, :] = jnp.zeros((16, 256), jnp.float32)
    terms = monomials()
    basis_rows = terms * 3 + [jnp.zeros((1, 256), jnp.float32)] * 14
    basis_ref[...] = jnp.concatenate(basis_rows, axis=0).astype(jnp.bfloat16)
    resid_rows_ref[...] = jnp.zeros_like(resid_rows_ref)
    flat = jnp.concatenate(terms + [jnp.zeros((1, 256), jnp.float32)] * 122, axis=0)
    for half in range(2):
        turned = flat[:, 128 * half : 128 * half + 128].T.astype(jnp.bfloat16)
        moment_ref[128 * half : 128 * half + 128, :] = turned
        moment_ref[256 + 128 * half : 384 + 128 * half, :] = turned

    low = low_half((1, 128))
    lane = lax.broadcasted_iota(jnp.int32, (1, 128), 1) & 63

    def forward(g, carry):
        index, keep, mid_x, mid_y = [], [], [], []
        for c in range(SEGS // 2):
            pair = []
            for half in range(2):
                n = SEGS * g + 2 * c + half
                t, place = seg_tile[n], seg_place[n]
                near = jnp.minimum(place, 15)
                row = lists_ref[pl.ds(t * 8 + (near >> 1), 1), :]
                row = jnp.where((near & 1) == half, row, swap(row))
                screen = ids_ref[0, t]
                pair.append(
                    (
                        row,
                        counts_ref[0, t] - place * SEG,
                        ((screen & 63) * 16 + 8).astype(jnp.float32),
                        ((screen >> 6) * 16 + 8).astype(jnp.float32),
                    )
                )
            index.append(jnp.where(low, pair[0][0], pair[1][0]))
            keep.append(lane < jnp.where(low, pair[0][1], pair[1][1]))
            mid_x.append(jnp.where(low, pair[0][2], pair[1][2]))
            mid_y.append(jnp.where(low, pair[0][3], pair[1][3]))
        index = jnp.concatenate(index, axis=1)
        keep = jnp.concatenate([jnp.where(part, 1.0, 0.0) for part in keep], axis=1) > 0.5
        mid_x = jnp.concatenate(mid_x, axis=1)
        mid_y = jnp.concatenate(mid_y, axis=1)
        index_ref[pl.ds(g, 1), :] = index
        found = gather_features(packed_ref, index)
        at_x = found[0] - mid_x
        at_y = found[1] - mid_y
        con_a, con_b, con_c, opacity = found[2:6]
        shape_ref[g, :, :] = jnp.concatenate([at_x, at_y, con_a, con_b, con_c, opacity, opacity, opacity], axis=0)
        line_x = -2.0 * con_a * at_x - con_b * at_y
        line_y = -2.0 * con_c * at_y - con_b * at_x
        level = opacity - 0.5 * (line_x * at_x + line_y * at_y)
        coefs = [jnp.where(keep, level, -30000.0)]
        coefs += [jnp.where(keep, row, 0.0) for row in (line_x, line_y, con_a, con_b, con_c)]
        for j in range(6):
            pieces = parts(coefs[j], 3)
            for step in range(3):
                coef_ref[6 * step + j : 6 * step + j + 1, :] = pieces[step].astype(jnp.float32)
        for k in range(3):
            coef_ref[18 + k : 19 + k, :] = found[6 + k]
        coef_ref[21:22, :] = index.astype(jnp.float32)
        first = pl.multiple_of(g * GROUP, GROUP)
        for c in range(GROUP // 128):
            wide_ref[pl.ds(first + 128 * c, 128), :] = coef_ref[:, 128 * c : 128 * c + 128].T
        rows = wide_ref[pl.ds(first, GROUP), :].astype(jnp.bfloat16)
        power = jnp.dot(rows, basis_ref[...], preferred_element_type=jnp.float32)
        power_ref[0, :, :] = power[:, :128]
        power_ref[1, :, :] = power[:, 128:]

        def block(b, state):
            transmit, red, green, blue = state
            for u in range(STEPS):
                i = b * STEPS + u
                here = pl.multiple_of(b * (STEPS * SEGS), STEPS * SEGS) + SEGS * u
                power = [power_ref[half, pl.ds(i, SEGS, stride=SEG), :] for half in range(2)]
                alpha = jnp.exp2(jnp.concatenate(power, axis=1))
                weight = alpha * transmit
                transmit = transmit - weight
                alpha_ref[pl.ds(first + here, SEGS), :] = alpha
                weight_ref[pl.ds(first + here, SEGS), :] = weight
                tint = wide_ref[pl.ds(first + i, SEGS, stride=SEG), :]
                red = red + weight * tint[:, 18:19]
                green = green + weight * tint[:, 19:20]
                blue = blue + weight * tint[:, 20:21]
            return (transmit, red, green, blue)

        zero = jnp.zeros((SEGS, 256), jnp.float32)
        transmit, *lights = lax.fori_loop(
            0, SEG // STEPS, block, (jnp.ones((SEGS, 256), jnp.float32), zero, zero, zero)
        )
        for s in range(SEGS):
            n = SEGS * g + s
            spot = seg_place[n] * 16 + seg_tile[n]
            pass_ref[pl.ds(spot, 1), :] = transmit[s : s + 1]
            for k in range(3):
                light_ref[k, pl.ds(spot, 1), :] = lights[k][s : s + 1]
        return carry

    lax.fori_loop(0, groups, forward, 0)

    transmit = jnp.ones((16, 256), jnp.float32)
    image = [jnp.zeros((16, 256), jnp.float32) for _ in range(3)]
    for place in range(16):
        span = slice(16 * place, 16 * place + 16)
        start_ref[span, :] = transmit
        image = [image[k] + transmit * light_ref[k, span, :] for k in range(3)]
        transmit = transmit * pass_ref[span, :]
    resid = []
    for k in range(3):
        image_ref[k] = image[k]
        resid.append(image[k] - target_ref[k])
        resid_ref[k] = resid[k]
    behind = jnp.zeros((16, 256), jnp.float32)
    for place in reversed(range(16)):
        span = slice(16 * place, 16 * place + 16)
        behind_ref[span, :] = behind
        own = sum(resid[k] * light_ref[k, span, :] for k in range(3))
        behind = own + pass_ref[span, :] * behind

    segment = lax.broadcasted_iota(jnp.int32, (SEGS, GROUP), 0)
    own_lane = segment == (lax.broadcasted_iota(jnp.int32, (SEGS, GROUP), 1) >> 6)

    def backward(g, carry):
        first = pl.multiple_of(g * GROUP, GROUP)
        tiles = [seg_tile[SEGS * g + s] for s in range(SEGS)]
        spots = [seg_place[SEGS * g + s] * 16 + tiles[s] for s in range(SEGS)]

        def rows_at(ref, places):
            return jnp.concatenate([ref[pl.ds(place, 1), :] for place in places], axis=0)

        start = rows_at(start_ref, spots)
        behind = rows_at(behind_ref, spots)
        resid = [rows_at(resid_ref.at[k], tiles) for k in range(3)]
        for k in range(3):
            high, rest = parts(resid[k], 2)
            resid_rows_ref[16 + 16 * k : 32 + 16 * k, :] = high.astype(jnp.float32)
            resid_rows_ref[64 + 16 * k : 80 + 16 * k, :] = rest.astype(jnp.float32)
        for half in range(2):
            turned = resid_rows_ref[:, 128 * half : 128 * half + 128].T.astype(jnp.bfloat16)
            moment_ref[512 + 128 * half : 640 + 128 * half, :] = turned
            moment_ref[768 + 128 * half : 896 + 128 * half, :] = turned

        def block(step, behind):
            b = SEG // STEPS - 1 - step
            at = pl.multiple_of(b * (STEPS * SEGS), STEPS * SEGS)
            for u in reversed(range(STEPS)):
                i = b * STEPS + u
                here = first + at + SEGS * u
                tint = wide_ref[pl.ds(first + i, SEGS, stride=SEG), :]
                shade = resid[0] * tint[:, 18:19] + resid[1] * tint[:, 19:20] + resid[2] * tint[:, 20:21]
                ahead = shade - behind
                behind = behind + alpha_ref[pl.ds(here, SEGS), :] * ahead
                weight = start * weight_ref[pl.ds(here, SEGS), :]
                for k, values in enumerate((weight * ahead, weight)):
                    high, rest = parts(values, 2)
                    pieces_ref[pl.ds(at + SEGS * u, SEGS), 512 * k : 512 * k + 256] = high
                    pieces_ref[pl.ds(at + SEGS * u, SEGS), 512 * k + 256 : 512 * k + 512] = rest
            return behind

        lax.fori_loop(0, SEG // STEPS, block, behind)
        sums_ref[...] = jnp.dot(pieces_ref[...], moment_ref[...], preferred_element_type=jnp.float32)
        turned = []
        for c in range(SEGS // 2):
            both = [sums_ref[pl.ds(2 * c + half, SEG, stride=SEGS), :] for half in range(2)]
            turned.append(jnp.concatenate(both, axis=0).T)
        turned = jnp.concatenate(turned, axis=1)
        m_0, m_x, m_y, m_xx, m_xy, m_yy = [LN2 * turned[j : j + 1] for j in range(6)]
        at_x, at_y, con_a, con_b, con_c = [shape_ref[g, j : j + 1, :] for j in range(5)]
        s_x = m_x - at_x * m_0
        s_y = m_y - at_y * m_0
        s_xx = m_xx - at_x * (m_x + s_x)
        s_xy = m_xy - at_x * m_y - at_y * s_x
        s_yy = m_yy - at_y * (m_y + s_y)
        rows = [
            -(2.0 * con_a * s_x + con_b * s_y),
            -(2.0 * con_c * s_y + con_b * s_x),
            s_xx,
            s_xy,
            s_yy,
            m_0,
        ]
        for k in range(3):
            both = turned[16 + 16 * k : 32 + 16 * k] + turned[64 + 16 * k : 80 + 16 * k]
            rows.append(jnp.sum(jnp.where(own_lane, both, 0.0), axis=0, keepdims=True))
        column = wide_ref[pl.ds(first, GROUP), :][:, 21:22]
        scatter_features(total_ref, rows, index_ref[pl.ds(g, 1), :], column)
        return carry

    lax.fori_loop(0, groups, backward, 0)
    unpack_total(total_ref, table_ref)
    table_to_blocks(table_ref, send_ref)


def smem():
    return pl.BlockSpec(memory_space=pltpu.SMEM)


def vmem():
    return pl.BlockSpec(memory_space=pltpu.VMEM)


def limits(mib):
    return pltpu.CompilerParams(vmem_limit_bytes=mib * 1024 * 1024)


def run_project(camera, gaussians):
    return pl.pallas_call(
        project_kernel,
        out_shape=jax.ShapeDtypeStruct((ROWS, 256), jnp.bfloat16),
        in_specs=[smem(), vmem()],
        out_specs=vmem(),
        scratch_shapes=[pltpu.VMEM((4096, 128), jnp.float32), pltpu.VMEM((FEATS, 64, 128), jnp.float32)],
        compiler_params=limits(16),
        name="project",
    )(camera, gaussians)


def run_fetch(parity, packed, asked):
    return pl.pallas_call(
        fetch_kernel,
        out_shape=(
            jax.ShapeDtypeStruct((64, 128), jnp.int32),
            jax.ShapeDtypeStruct((640, 128), jnp.float32),
        ),
        in_specs=[smem(), vmem(), vmem()],
        out_specs=(vmem(), vmem()),
        scratch_shapes=[pltpu.VMEM((FEATS, 64, 128), jnp.float32)],
        compiler_params=limits(16),
        name="fetch",
    )(parity, packed, asked)


def run_render(tile_ids, counts, active, received, lists, target):
    f32, bf16 = jnp.float32, jnp.bfloat16
    entries = MAX_GROUPS * GROUP
    return pl.pallas_call(
        render_kernel,
        out_shape=(
            jax.ShapeDtypeStruct((3, 16, 256), f32),
            jax.ShapeDtypeStruct((640, 128), f32),
        ),
        in_specs=[smem(), smem(), smem(), vmem(), vmem(), vmem()],
        out_specs=(vmem(), vmem()),
        scratch_shapes=[
            pltpu.SMEM((SEGS * MAX_GROUPS,), jnp.int32),
            pltpu.SMEM((SEGS * MAX_GROUPS,), jnp.int32),
            pltpu.VMEM((FEATS, 64, 128), f32),
            pltpu.VMEM((ROWS, 256), bf16),
            pltpu.VMEM((BACK_ROWS, 256), f32),
            pltpu.VMEM((32, 256), bf16),
            pltpu.VMEM((1024, 128), bf16),
            pltpu.VMEM((16, GROUP), jnp.int32),
            pltpu.VMEM((MAX_GROUPS, 8, GROUP), f32),
            pltpu.VMEM((32, GROUP), f32),
            pltpu.VMEM((entries, 32), f32),
            pltpu.VMEM((2, GROUP, 128), f32),
            pltpu.VMEM((entries, 256), f32),
            pltpu.VMEM((entries, 256), f32),
            pltpu.VMEM((272, 256), f32),
            pltpu.VMEM((3, 272, 256), f32),
            pltpu.VMEM((272, 256), f32),
            pltpu.VMEM((272, 256), f32),
            pltpu.VMEM((3, 16, 256), f32),
            pltpu.VMEM((128, 256), f32),
            pltpu.VMEM((GROUP, 1024), bf16),
            pltpu.VMEM((GROUP, 128), f32),
        ],
        compiler_params=limits(48),
        name="render",
    )(tile_ids, counts, active, received, lists, target)


def run_return(camera, gaussians, index, back):
    return pl.pallas_call(
        return_kernel,
        out_shape=jax.ShapeDtypeStruct((59, 8192), jnp.float32),
        in_specs=[smem(), vmem(), vmem(), vmem()],
        out_specs=vmem(),
        scratch_shapes=[
            pltpu.VMEM((4096, 128), jnp.float32),
            pltpu.VMEM((FEATS, 64, 128), jnp.float32),
            pltpu.VMEM((BACK_ROWS, 256), jnp.float32),
        ],
        compiler_params=limits(24),
        name="give_back",
    )(camera, gaussians, index, back)


def exchange(rows):
    count = rows.shape[0] // 128 * rows.shape[1]
    moved = lax.all_to_all(rows.reshape(128, 1, count), AXES, split_axis=0, concat_axis=0, tiled=True)
    return moved.reshape(rows.shape)


def local(gaussians, camera, asked, parity, tile_ids, tile_lists, tile_counts, tile_active, target, send_on):
    lists = tile_lists.reshape(128, 128)
    packed = run_project(camera, gaussians)
    index, send = run_fetch(parity, packed, asked)
    image, back = run_render(tile_ids, tile_counts, tile_active, send_on(send), lists, target)
    grads = run_return(camera, gaussians, index, send_on(back))
    return (image, grads)


def per_device(gaussians, camera, fetch_index, tile_ids, tile_lists, tile_counts, tile_active, target):
    asked = exchange(jnp.repeat(fetch_index.reshape(64, 128), 2, axis=0))
    parity = (lax.axis_index("shard") % 2).astype(jnp.int32).reshape(1)
    return local(gaussians, camera, asked, parity, tile_ids, tile_lists, tile_counts, tile_active, target, exchange)


def solution(mesh):
    in_specs = (
        P(None, AXES),
        P(),
        P(AXES, None),
        P(AXES, None),
        P(AXES, None, None),
        P(AXES, None),
        P(AXES, None),
        P(None, AXES, None),
    )
    out_specs = (P(None, AXES, None), P(None, AXES))
    return jax.shard_map(per_device, mesh=mesh, in_specs=in_specs, out_specs=out_specs, check_vma=False)
```

time: 1670 us -> 122 us (0.07); the launches traced: 1650 us -> 122 us
  other arithmetic: 744 us -> 0 us
  local copies, waits for them, and re-layouts: 487 us -> 3.75 us
  matrix products: 253 us -> 0 us
  loops' own time: 77.1 us -> 0 us
  Pallas kernels: 0 us -> 62.4 us
    another operation x663 -> x0, other arithmetic: 276 us -> none
    dot_general x192 -> x0, matrix products: 253 us -> none  [advance(): jnp.dot(cols[6:9], weights, precision=lax.Precision.HIGHEST)]
    scatter-add x17 -> x0, other arithmetic: 217 us -> none  [the longest x16 171 us: tile_pass(): picked = features[:, entries].reshape(9, blocks, SPAN).transpose(1, 0, 2)]
    gather x17 -> x0, local copies, waits for them, and re-layouts: 110 us -> none  [the longest x16 79.8 us: tile_pass(): picked = features[:, entries].reshape(9, blocks, SPAN).transpose(1, 0, 2)]
    dynamic_update_slice x160 -> x0, local copies, waits for them, and re-layouts: 86.8 us -> none  [the longest x96 83.3 us: total(): lax.map(one_tile, (tiles, entries, counts, live, goal.transpose(1, 0, 2)))]
    another operation x34 -> x0, loops' own time: 77.1 us -> none  [the longest x2 56.8 us: total(): lax.map(one_tile, (tiles, entries, counts, live, goal.transpose(1, 0, 2)))]
    dynamic_update_slice x112 -> x0, other arithmetic: 64.1 us -> none  [the longest x48 62.5 us: total(): lax.map(one_tile, (tiles, entries, counts, live, goal.transpose(1, 0, 2)))]
    dynamic_slice x208 -> x0, local copies, waits for them, and re-layouts: 63.8 us -> none  [the longest x80 62.5 us: total(): lax.map(one_tile, (tiles, entries, counts, live, goal.transpose(1, 0, 2)))]
where the time goes in v1:
time: 122 us
  Pallas kernels  62.4 us (51%)
  blocking collectives  21 us (17%)
  waiting for transfers between devices  18.1 us (15%)
  starting transfers between devices  15.6 us (13%)
  local copies, waits for them, and re-layouts  3.75 us (3%)
    pallas_call x1, Pallas kernels, run_render(): pl.pallas_call(render_kernel, out_shape=(jax.ShapeDtypeStruct((3, 16, 256...  47.8 us
    all_to_all x1, blocking collectives, exchange(): lax.all_to_all(rows.reshape(128, 1, count), AXES, split_axis=0, concat_ax...  21 us
    all_to_all x2, waiting for transfers between devices, exchange(): lax.all_to_all(rows.reshape(128, 1, count), AXES, split_axis=0, concat_ax...  18.1 us
    all_to_all x2, starting transfers between devices, exchange(): lax.all_to_all(rows.reshape(128, 1, count), AXES, split_axis=0, concat_ax...  15.6 us
    pallas_call x1, Pallas kernels, run_return(): pl.pallas_call(return_kernel, out_shape=jax.ShapeDtypeStruct((59, 8192),...  6.63 us
    pallas_call x1, Pallas kernels, run_fetch(): pl.pallas_call(fetch_kernel, out_shape=(jax.ShapeDtypeStruct((64, 128), j...  6.59 us
  transfers between devices with their start and end apart: 2, of which 2 were waited for; matrix products, arithmetic and copies ran while one was open for 0% of the time, Pallas kernels for 1%

profile of v1, /device:TPU:1, one launch (start us, length us, event | category | flops | bytes accessed | tf_op | source)
XLA Modules:
  0.0 121.6 jit_solution(1714898863694555714)
XLA Ops:
  0.6 0.0 copy-start.8
  0.6 0.0 copy-start.2
  0.7 0.0 copy-start.7
  0.7 0.0 copy-start.6
  0.7 0.0 copy-start.5
  0.7 1.5 %broadcast_in_dim.3 = s32[64,2,128]{2,1,0:T(2,128)} broadcast(s32[64,128]{1,0:T(8,128)} %bitcast.12), dimensions={0,2} | broadcast | bytes 98304 | tf_op jit(solution)/shard_map/broadcast_in_dim | solution.py:681
  2.1 11.5 %all-to-all-start = ((s32[128,1,128]{2,1,0:T(1,128)}), s32[128,1,128]{2,1,0:T(1,128)S(1)}, u32[]{:S(2)}, u32[]{:S(2)}) async-start(s32[128,1,128]{2,1,0:T(1,128)} %bitcast.2), calls=%async_computation | async-start | bytes 131072 | tf_op jit(solution)/shard_map/all_to_all | solution.py:667
  13.7 0.0 copy-start
  13.7 1.6 %copy-done = f32[59,8192]{1,0:T(8,128)S(1)} copy-done((f32[59,8192]{1,0:T(8,128)S(1)}, f32[59,8192]{1,0:T(8,128)}, u32[]{:S(2)}) %copy-start) | copy-done | bytes 1933336
  15.3 0.0 copy-start.3
  15.3 0.7 copy-done.3
  15.9 0.0 copy-start.1
  15.9 0.0 copy-start.4
  15.9 1.4 %project.1.packed_ref = bf16[640,256]{1,0:T(8,128)(2,1)S(1)} custom-call(f32[4]{0:T(128)S(1)} %copy-done.3, f32[59,8192]{1,0:T(8,128)S(1)} %copy-done), custom_call_target="tpu_custom_call" | custom-call | tf_op jit(solution)/shard_map/project/pallas_call | solution.py:583
  17.3 6.1 %all-to-all-done = s32[128,1,128]{2,1,0:T(1,128)S(1)} async-done(((s32[128,1,128]{2,1,0:T(1,128)}), s32[128,1,128]{2,1,0:T(1,128)S(1)}, u32[]{:S(2)}, u32[]{:S(2)}) %all-to-all-start) | async-done | bytes 65568 | tf_op jit(solution)/shard_map/all_to_all | solution.py:667
  23.5 6.6 %fetch.1 = (s32[64,128]{1,0:T(8,128)S(1)}, f32[640,128]{1,0:T(8,128)}) custom-call(s32[1]{0:T(128)} %bitcast.parity_ref, bf16[640,256]{1,0:T(8,128)(2,1)S(1)} %project.1.packed_ref, s32[128,128]{1,0:T(8,128)S(1)} %bitcast.11), custom_call_target="tpu_custom_call" | custom-call | tf_op jit(solution)/shard_map/fetch/pallas_call | solution.py:595
  30.1 4.1 %all-to-all-start.1 = ((f32[128,1,640]{2,1,0:T(1,128)}), f32[128,1,640]{2,1,0:T(1,128)S(1)}, u32[]{:S(2)}, u32[]{:S(2)}) async-start(f32[128,1,640]{2,1,0:T(1,128)} %bitcast.4), calls=%async_computation.1 | async-start | bytes 655360 | tf_op jit(solution)/shard_map/all_to_all | solution.py:667
  34.1 0.0 copy-done.8
  34.2 12.0 %all-to-all-done.1 = f32[128,1,640]{2,1,0:T(1,128)S(1)} async-done(((f32[128,1,640]{2,1,0:T(1,128)}), f32[128,1,640]{2,1,0:T(1,128)S(1)}, u32[]{:S(2)}, u32[]{:S(2)}) %all-to-all-start.1) | async-done | bytes 327712 | tf_op jit(solution)/shard_map/all_to_all | solution.py:667
  46.1 0.0 copy-done.2
  46.1 0.0 copy-done.7
  46.1 0.0 copy-done.6
  46.2 0.0 copy-done.5
  46.2 47.8 %render.1 = (f32[3,16,256]{2,1,0:T(8,128)}, f32[640,128]{1,0:T(8,128)S(1)}) custom-call(s32[1,16]{1,0:T(1,128)S(1)} %copy-done.5, s32[1,16]{1,0:T(1,128)S(1)} %copy-done.6, s32[1,16]{1,0:T(1,128)S(1)} %copy-done.7, f32[640,128]{1,0:T(8,128)S(1)} %bitcast.9, s32[128,128]{1,0:T(8,128)S(1)} %reshape.33.lists_ref, f32[3,16,256]{2,1,0:T(8,128)S(1)} %copy-done.2), custom_call_target="tpu_custom_call" | custom-call | tf_op jit(solution)/shard_map/render/pallas_call | solution.py:612
  93.9 21.0 %all_to_all.15 = f32[128,1,640]{2,1,0:T(1,128)S(1)} all-to-all(f32[128,1,640]{2,1,0:T(1,128)S(1)} %bitcast.10), channel_id=1, replica_groups=mesh['tile'=32,'shard'=4] {'tile','shard'}, dimensions={0} | all-to-all | bytes 655360 | tf_op jit(solution)/shard_map/all_to_all | solution.py:667
  114.9 0.0 copy-done.1
  114.9 0.0 copy-done.4
  114.9 6.6 %give_back.1 = f32[59,8192]{1,0:T(8,128)} custom-call(f32[4]{0:T(128)S(1)} %copy-done.4, f32[59,8192]{1,0:T(8,128)S(1)} %copy-done.1, s32[64,128]{1,0:T(8,128)S(1)} %get-tuple-element.8.index_ref, f32[640,128]{1,0:T(8,128)S(1)} %bitcast.8), custom_call_target="tpu_custom_call" | custom-call | tf_op jit(solution)/shard_map/give_back/pallas_call | solution.py:650
  (1 shorter events, 0.0 us)
Async XLA Ops:
  0.6 33.5 %copy-start.8 = (s32[1,16,1024]{2,1,0:T(8,128)S(1)}, s32[1,16,1024]{2,1,0:T(8,128)}, u32[]{:S(2)}) copy-start(s32[1,16,1024]{2,1,0:T(8,128)} %param.12) | copy-start | bytes 196612
  0.6 45.5 %copy-start.2 = (f32[3,16,256]{2,1,0:T(8,128)S(1)}, f32[3,16,256]{2,1,0:T(8,128)}, u32[]{:S(2)}) copy-start(f32[3,16,256]{2,1,0:T(8,128)} %target_ref.1) | copy-start | bytes 147460
  0.7 45.5 %copy-start.7 = (s32[1,16]{1,0:T(1,128)S(1)}, s32[1,16]{1,0:T(1,128)}, u32[]{:S(2)}) copy-start(s32[1,16]{1,0:T(1,128)} %active_ref.1) | copy-start | bytes 196
  0.7 45.5 %copy-start.6 = (s32[1,16]{1,0:T(1,128)S(1)}, s32[1,16]{1,0:T(1,128)}, u32[]{:S(2)}) copy-start(s32[1,16]{1,0:T(1,128)} %counts_ref.1) | copy-start | bytes 196
  0.7 45.5 %copy-start.5 = (s32[1,16]{1,0:T(1,128)S(1)}, s32[1,16]{1,0:T(1,128)}, u32[]{:S(2)}) copy-start(s32[1,16]{1,0:T(1,128)} %ids_ref.1) | copy-start | bytes 196
  2.1 21.3 %all-to-all-start = ((s32[128,1,128]{2,1,0:T(1,128)}), s32[128,1,128]{2,1,0:T(1,128)S(1)}, u32[]{:S(2)}, u32[]{:S(2)}) async-start(s32[128,1,128]{2,1,0:T(1,128)} %bitcast.2), calls=%async_computation | async-start | bytes 131072 | tf_op jit(solution)/shard_map/all_to_all | solution.py:667
  13.7 1.6 %copy-start = (f32[59,8192]{1,0:T(8,128)S(1)}, f32[59,8192]{1,0:T(8,128)}, u32[]{:S(2)}) copy-start(f32[59,8192]{1,0:T(8,128)} %gaussians_ref.3) | copy-start | bytes 5799940
  15.3 0.7 copy-start.3
  15.9 99.0 %copy-start.1 = (f32[59,8192]{1,0:T(8,128)S(1)}, f32[59,8192]{1,0:T(8,128)}, u32[]{:S(2)}) copy-start(f32[59,8192]{1,0:T(8,128)} %gaussians_ref.3) | copy-start | bytes 5799940
  15.9 99.0 %copy-start.4 = (f32[4]{0:T(128)S(1)}, f32[4]{0:T(128)}, u32[]{:S(2)}) copy-start(f32[4]{0:T(128)} %camera_ref.3) | copy-start | bytes 52
  30.1 16.1 %all-to-all-start.1 = ((f32[128,1,640]{2,1,0:T(1,128)}), f32[128,1,640]{2,1,0:T(1,128)S(1)}, u32[]{:S(2)}, u32[]{:S(2)}) async-start(f32[128,1,640]{2,1,0:T(1,128)} %bitcast.4), calls=%async_computation.1 | async-start | bytes 655360 | tf_op jit(solution)/shard_map/all_to_all | solution.py:667

commit v2 on v1

--- a/solution.py
+++ b/solution.py
@@ -12,7 +12,6 @@
 SEGS = 16
 GROUP = SEG * SEGS
 MAX_GROUPS = 9
-STEPS = 16
 LOG2E = 1.4426950408889634
 LN2 = 0.6931471805599453
 FEATS = 9
@@ -264,14 +263,11 @@
         jnp.where(low, swap(even), odd),
     )
 
-    def body(q, carry):
+    for q in range(16):
         rows = gather_features(packed_ref, row_of(index_ref, q))
         for f in range(FEATS):
             for c in range(4):
-                table_ref[f, pl.ds(4 * q + c, 1), :] = rows[f][:, 128 * c : 128 * c + 128]
-        return carry
-
-    lax.fori_loop(0, 16, body, 0)
+                table_ref[f, 4 * q + c : 4 * q + c + 1, :] = rows[f][:, 128 * c : 128 * c + 128]
     table_to_blocks(table_ref, send_ref)
 
 
@@ -317,27 +313,51 @@
     return [jnp.ones((1, 256), jnp.float32), x, y, x * x, x * y, y * y]
 
 
+def plan_kernel(counts_ref, active_ref, after_ref, seg_tile, seg_place, groups_ref):
+    def clear(n, carry):
+        seg_tile[n] = 0
+        seg_place[n] = 16
+        return carry
+
+    lax.fori_loop(0, SEGS * (MAX_GROUPS + 1), clear, 0)
+
+    def add_tile(t, n):
+        used = jnp.where(active_ref[0, t] > 0, (counts_ref[0, t] + (SEG - 1)) >> 6, 0)
+
+        def add_segment(k, m):
+            seg_tile[m] = t
+            seg_place[m] = k
+            return m + 1
+
+        return lax.fori_loop(0, used, add_segment, n)
+
+    segments = lax.fori_loop(0, 16, add_tile, 0)
+    groups_ref[0] = (segments + (SEGS - 1)) // SEGS
+
+
 def render_kernel(
     ids_ref,
     counts_ref,
-    active_ref,
+    seg_tile,
+    seg_place,
+    groups_ref,
     recv_ref,
     lists_ref,
     target_ref,
     image_ref,
     send_ref,
-    seg_tile,
-    seg_place,
     table_ref,
     packed_ref,
     total_ref,
     basis_ref,
     moment_ref,
-    index_ref,
-    shape_ref,
     coef_ref,
+    plain_ref,
     wide_ref,
-    power_ref,
+    power_a_ref,
+    power_b_ref,
+    tint_a_ref,
+    tint_b_ref,
     alpha_ref,
     weight_ref,
     pass_ref,
@@ -345,30 +365,10 @@
     start_ref,
     behind_ref,
     resid_ref,
-    resid_rows_ref,
-    pieces_ref,
-    sums_ref,
+    pieces_a_ref,
+    pieces_b_ref,
 ):
-    def clear(n, carry):
-        seg_tile[n] = 0
-        seg_place[n] = 16
-        return carry
-
-    lax.fori_loop(0, SEGS * MAX_GROUPS, clear, 0)
-
-    def add_tile(t, n):
-        used = jnp.where(active_ref[0, t] > 0, (counts_ref[0, t] + (SEG - 1)) >> 6, 0)
-
-        def add_segment(k, m):
-            seg_tile[m] = t
-            seg_place[m] = k
-            return m + 1
-
-        return lax.fori_loop(0, used, add_segment, n)
-
-    segments = lax.fori_loop(0, 16, add_tile, 0)
-    groups = (segments + (SEGS - 1)) // SEGS
-
+    groups = groups_ref[0]
     blocks_to_table(recv_ref, table_ref)
     pack_table(table_ref, packed_ref)
     total_ref[...] = jnp.zeros_like(total_ref)
@@ -380,17 +380,13 @@
     terms = monomials()
     basis_rows = terms * 3 + [jnp.zeros((1, 256), jnp.float32)] * 14
     basis_ref[...] = jnp.concatenate(basis_rows, axis=0).astype(jnp.bfloat16)
-    resid_rows_ref[...] = jnp.zeros_like(resid_rows_ref)
-    flat = jnp.concatenate(terms + [jnp.zeros((1, 256), jnp.float32)] * 122, axis=0)
-    for half in range(2):
-        turned = flat[:, 128 * half : 128 * half + 128].T.astype(jnp.bfloat16)
-        moment_ref[128 * half : 128 * half + 128, :] = turned
-        moment_ref[256 + 128 * half : 384 + 128 * half, :] = turned
+    flat = jnp.concatenate(terms + [jnp.zeros((1, 256), jnp.float32)] * 10, axis=0)
+    moment_ref[...] = jnp.concatenate([flat, flat], axis=1).astype(jnp.bfloat16)
 
     low = low_half((1, 128))
     lane = lax.broadcasted_iota(jnp.int32, (1, 128), 1) & 63
 
-    def forward(g, carry):
+    def prepare(g, power_ref, tint_ref):
         index, keep, mid_x, mid_y = [], [], [], []
         for c in range(SEGS // 2):
             pair = []
@@ -417,12 +413,10 @@
         keep = jnp.concatenate([jnp.where(part, 1.0, 0.0) for part in keep], axis=1) > 0.5
         mid_x = jnp.concatenate(mid_x, axis=1)
         mid_y = jnp.concatenate(mid_y, axis=1)
-        index_ref[pl.ds(g, 1), :] = index
         found = gather_features(packed_ref, index)
         at_x = found[0] - mid_x
         at_y = found[1] - mid_y
         con_a, con_b, con_c, opacity = found[2:6]
-        shape_ref[g, :, :] = jnp.concatenate([at_x, at_y, con_a, con_b, con_c, opacity, opacity, opacity], axis=0)
         line_x = -2.0 * con_a * at_x - con_b * at_y
         line_y = -2.0 * con_c * at_y - con_b * at_x
         level = opacity - 0.5 * (line_x * at_x + line_y * at_y)
@@ -435,44 +429,52 @@
         for k in range(3):
             coef_ref[18 + k : 19 + k, :] = found[6 + k]
         coef_ref[21:22, :] = index.astype(jnp.float32)
+        for j, row in enumerate((at_x, at_y, con_a, con_b, con_c)):
+            coef_ref[22 + j : 23 + j, :] = row
         first = pl.multiple_of(g * GROUP, GROUP)
         for c in range(GROUP // 128):
-            wide_ref[pl.ds(first + 128 * c, 128), :] = coef_ref[:, 128 * c : 128 * c + 128].T
-        rows = wide_ref[pl.ds(first, GROUP), :].astype(jnp.bfloat16)
-        power = jnp.dot(rows, basis_ref[...], preferred_element_type=jnp.float32)
-        power_ref[0, :, :] = power[:, :128]
-        power_ref[1, :, :] = power[:, 128:]
-
-        def block(b, state):
-            transmit, red, green, blue = state
-            for u in range(STEPS):
-                i = b * STEPS + u
-                here = pl.multiple_of(b * (STEPS * SEGS), STEPS * SEGS) + SEGS * u
-                power = [power_ref[half, pl.ds(i, SEGS, stride=SEG), :] for half in range(2)]
-                alpha = jnp.exp2(jnp.concatenate(power, axis=1))
-                weight = alpha * transmit
-                transmit = transmit - weight
-                alpha_ref[pl.ds(first + here, SEGS), :] = alpha
-                weight_ref[pl.ds(first + here, SEGS), :] = weight
-                tint = wide_ref[pl.ds(first + i, SEGS, stride=SEG), :]
-                red = red + weight * tint[:, 18:19]
-                green = green + weight * tint[:, 19:20]
-                blue = blue + weight * tint[:, 20:21]
-            return (transmit, red, green, blue)
-
+            plain_ref[128 * c : 128 * c + 128, :] = coef_ref[:, 128 * c : 128 * c + 128].T
+        turned = jnp.concatenate([plain_ref[pl.ds(i, SEGS, stride=SEG), :] for i in range(SEG)], axis=0)
+        wide_ref[pl.ds(first, GROUP), :] = turned
+        tint_ref[...] = turned
+        power = jnp.dot(turned.astype(jnp.bfloat16), basis_ref[...], preferred_element_type=jnp.float32)
+        power_ref[...] = power
+
+    def forward(g, power_ref, tint_ref):
+        first = pl.multiple_of(g * GROUP, GROUP)
         zero = jnp.zeros((SEGS, 256), jnp.float32)
-        transmit, *lights = lax.fori_loop(
-            0, SEG // STEPS, block, (jnp.ones((SEGS, 256), jnp.float32), zero, zero, zero)
-        )
+        transmit = jnp.ones((SEGS, 256), jnp.float32)
+        lights = [zero, zero, zero]
+        for i in range(SEG):
+            alpha = jnp.exp2(power_ref[SEGS * i : SEGS * i + SEGS, :])
+            weight = alpha * transmit
+            transmit = transmit - weight
+            alpha_ref[pl.ds(first + SEGS * i, SEGS), :] = alpha
+            weight_ref[pl.ds(first + SEGS * i, SEGS), :] = weight
+            tint = tint_ref[SEGS * i : SEGS * i + SEGS, :]
+            lights = [lights[k] + weight * tint[:, 18 + k : 19 + k] for k in range(3)]
         for s in range(SEGS):
             n = SEGS * g + s
             spot = seg_place[n] * 16 + seg_tile[n]
             pass_ref[pl.ds(spot, 1), :] = transmit[s : s + 1]
             for k in range(3):
                 light_ref[k, pl.ds(spot, 1), :] = lights[k][s : s + 1]
+
+    buffers = ((power_a_ref, tint_a_ref), (power_b_ref, tint_b_ref))
+
+    def forward_pair(p, carry):
+        prepare(2 * p + 1, *buffers[1])
+        forward(2 * p, *buffers[0])
+        prepare(2 * p + 2, *buffers[0])
+        forward(2 * p + 1, *buffers[1])
         return carry
 
-    lax.fori_loop(0, groups, forward, 0)
+    prepare(0, *buffers[0])
+    lax.fori_loop(0, groups >> 1, forward_pair, 0)
+
+    @pl.when((groups & 1) == 1)
+    def _():
+        forward(groups - 1, *buffers[0])
 
     transmit = jnp.ones((16, 256), jnp.float32)
     image = [jnp.zeros((16, 256), jnp.float32) for _ in range(3)]
@@ -494,54 +496,44 @@
         behind = own + pass_ref[span, :] * behind
 
     segment = lax.broadcasted_iota(jnp.int32, (SEGS, GROUP), 0)
-    own_lane = segment == (lax.broadcasted_iota(jnp.int32, (SEGS, GROUP), 1) >> 6)
-
-    def backward(g, carry):
+    own_lane = segment == (lax.broadcasted_iota(jnp.int32, (SEGS, GROUP), 1) & (SEGS - 1))
+
+    def rows_at(ref, places):
+        return jnp.concatenate([ref[pl.ds(place, 1), :] for place in places], axis=0)
+
+    def backward(g, pieces_ref):
         first = pl.multiple_of(g * GROUP, GROUP)
         tiles = [seg_tile[SEGS * g + s] for s in range(SEGS)]
         spots = [seg_place[SEGS * g + s] * 16 + tiles[s] for s in range(SEGS)]
-
-        def rows_at(ref, places):
-            return jnp.concatenate([ref[pl.ds(place, 1), :] for place in places], axis=0)
-
         start = rows_at(start_ref, spots)
         behind = rows_at(behind_ref, spots)
         resid = [rows_at(resid_ref.at[k], tiles) for k in range(3)]
-        for k in range(3):
-            high, rest = parts(resid[k], 2)
-            resid_rows_ref[16 + 16 * k : 32 + 16 * k, :] = high.astype(jnp.float32)
-            resid_rows_ref[64 + 16 * k : 80 + 16 * k, :] = rest.astype(jnp.float32)
-        for half in range(2):
-            turned = resid_rows_ref[:, 128 * half : 128 * half + 128].T.astype(jnp.bfloat16)
-            moment_ref[512 + 128 * half : 640 + 128 * half, :] = turned
-            moment_ref[768 + 128 * half : 896 + 128 * half, :] = turned
-
-        def block(step, behind):
-            b = SEG // STEPS - 1 - step
-            at = pl.multiple_of(b * (STEPS * SEGS), STEPS * SEGS)
-            for u in reversed(range(STEPS)):
-                i = b * STEPS + u
-                here = first + at + SEGS * u
-                tint = wide_ref[pl.ds(first + i, SEGS, stride=SEG), :]
-                shade = resid[0] * tint[:, 18:19] + resid[1] * tint[:, 19:20] + resid[2] * tint[:, 20:21]
-                ahead = shade - behind
-                behind = behind + alpha_ref[pl.ds(here, SEGS), :] * ahead
-                weight = start * weight_ref[pl.ds(here, SEGS), :]
-                for k, values in enumerate((weight * ahead, weight)):
-                    high, rest = parts(values, 2)
-                    pieces_ref[pl.ds(at + SEGS * u, SEGS), 512 * k : 512 * k + 256] = high
-                    pieces_ref[pl.ds(at + SEGS * u, SEGS), 512 * k + 256 : 512 * k + 512] = rest
-            return behind
-
-        lax.fori_loop(0, SEG // STEPS, block, behind)
-        sums_ref[...] = jnp.dot(pieces_ref[...], moment_ref[...], preferred_element_type=jnp.float32)
-        turned = []
-        for c in range(SEGS // 2):
-            both = [sums_ref[pl.ds(2 * c + half, SEG, stride=SEGS), :] for half in range(2)]
-            turned.append(jnp.concatenate(both, axis=0).T)
-        turned = jnp.concatenate(turned, axis=1)
-        m_0, m_x, m_y, m_xx, m_xy, m_yy = [LN2 * turned[j : j + 1] for j in range(6)]
-        at_x, at_y, con_a, con_b, con_c = [shape_ref[g, j : j + 1, :] for j in range(5)]
+        for i in reversed(range(SEG)):
+            here = first + SEGS * i
+            tint = wide_ref[pl.ds(here, SEGS), :]
+            shade = resid[0] * tint[:, 18:19] + resid[1] * tint[:, 19:20] + resid[2] * tint[:, 20:21]
+            ahead = shade - behind
+            behind = behind + alpha_ref[pl.ds(here, SEGS), :] * ahead
+            weight = start * weight_ref[pl.ds(here, SEGS), :]
+            for k, values in enumerate((weight * ahead, weight)):
+                high, rest = parts(values, 2)
+                pieces_ref[SEGS * i : SEGS * i + SEGS, 512 * k : 512 * k + 256] = high
+                pieces_ref[SEGS * i : SEGS * i + SEGS, 512 * k + 256 : 512 * k + 512] = rest
+
+    def across(left, right):
+        return lax.dot_general(left, right, (((1,), (1,)), ((), ())), preferred_element_type=jnp.float32)
+
+    def collect(g, pieces_ref):
+        first = pl.multiple_of(g * GROUP, GROUP)
+        wide = wide_ref[pl.ds(first, GROUP), :]
+        known = jnp.concatenate([wide[128 * c : 128 * c + 128].T for c in range(GROUP // 128)], axis=1)
+        tiles = [seg_tile[SEGS * g + s] for s in range(SEGS)]
+        resid = [parts(rows_at(resid_ref.at[k], tiles), 2) for k in range(3)]
+        resid = jnp.concatenate([resid[k][step] for step in range(2) for k in range(3)], axis=0)
+        moments = across(moment_ref[...], pieces_ref[:, 0:512])
+        light = across(jnp.concatenate([resid, resid], axis=1), pieces_ref[:, 512:1024])
+        m_0, m_x, m_y, m_xx, m_xy, m_yy = [LN2 * moments[j : j + 1] for j in range(6)]
+        at_x, at_y, con_a, con_b, con_c = [known[22 + j : 23 + j] for j in range(5)]
         s_x = m_x - at_x * m_0
         s_y = m_y - at_y * m_0
         s_xx = m_xx - at_x * (m_x + s_x)
@@ -556,13 +548,24 @@
             m_0,
         ]
         for k in range(3):
-            both = turned[16 + 16 * k : 32 + 16 * k] + turned[64 + 16 * k : 80 + 16 * k]
+            both = light[16 * k : 16 * k + 16] + light[48 + 16 * k : 64 + 16 * k]
             rows.append(jnp.sum(jnp.where(own_lane, both, 0.0), axis=0, keepdims=True))
-        column = wide_ref[pl.ds(first, GROUP), :][:, 21:22]
-        scatter_features(total_ref, rows, index_ref[pl.ds(g, 1), :], column)
+        scatter_features(total_ref, rows, known[21:22].astype(jnp.int32), wide[:, 21:22])
+
+    def backward_pair(p, carry):
+        backward(2 * p + 1, pieces_b_ref)
+        collect(2 * p, pieces_a_ref)
+        backward(2 * p + 2, pieces_a_ref)
+        collect(2 * p + 1, pieces_b_ref)
         return carry
 
-    lax.fori_loop(0, groups, backward, 0)
+    backward(0, pieces_a_ref)
+    lax.fori_loop(0, groups >> 1, backward_pair, 0)
+
+    @pl.when((groups & 1) == 1)
+    def _():
+        collect(groups - 1, pieces_a_ref)
+
     unpack_total(total_ref, table_ref)
     table_to_blocks(table_ref, send_ref)
 
@@ -606,30 +609,41 @@
     )(parity, packed, asked)
 
 
-def run_render(tile_ids, counts, active, received, lists, target):
+def run_plan(counts, active, after):
+    segments = jax.ShapeDtypeStruct((SEGS * (MAX_GROUPS + 1),), jnp.int32)
+    return pl.pallas_call(
+        plan_kernel,
+        out_shape=(segments, segments, jax.ShapeDtypeStruct((1,), jnp.int32)),
+        in_specs=[smem(), smem(), pl.BlockSpec(memory_space=pl.ANY)],
+        out_specs=(smem(), smem(), smem()),
+        name="plan",
+    )(counts, active, after)
+
+
+def run_render(tile_ids, counts, segments, received, lists, target):
     f32, bf16 = jnp.float32, jnp.bfloat16
-    entries = MAX_GROUPS * GROUP
+    entries = (MAX_GROUPS + 1) * GROUP
     return pl.pallas_call(
         render_kernel,
         out_shape=(
             jax.ShapeDtypeStruct((3, 16, 256), f32),
             jax.ShapeDtypeStruct((640, 128), f32),
         ),
-        in_specs=[smem(), smem(), smem(), vmem(), vmem(), vmem()],
+        in_specs=[smem()] * 5 + [vmem()] * 3,
         out_specs=(vmem(), vmem()),
         scratch_shapes=[
-            pltpu.SMEM((SEGS * MAX_GROUPS,), jnp.int32),
-            pltpu.SMEM((SEGS * MAX_GROUPS,), jnp.int32),
             pltpu.VMEM((FEATS, 64, 128), f32),
             pltpu.VMEM((ROWS, 256), bf16),
             pltpu.VMEM((BACK_ROWS, 256), f32),
             pltpu.VMEM((32, 256), bf16),
-            pltpu.VMEM((1024, 128), bf16),
-            pltpu.VMEM((16, GROUP), jnp.int32),
-            pltpu.VMEM((MAX_GROUPS, 8, GROUP), f32),
+            pltpu.VMEM((16, 512), bf16),
             pltpu.VMEM((32, GROUP), f32),
+            pltpu.VMEM((GROUP, 32), f32),
             pltpu.VMEM((entries, 32), f32),
-            pltpu.VMEM((2, GROUP, 128), f32),
+            pltpu.VMEM((GROUP, 256), f32),
+            pltpu.VMEM((GROUP, 256), f32),
+            pltpu.VMEM((GROUP, 32), f32),
+            pltpu.VMEM((GROUP, 32), f32),
             pltpu.VMEM((entries, 256), f32),
             pltpu.VMEM((entries, 256), f32),
             pltpu.VMEM((272, 256), f32),
@@ -637,13 +651,12 @@
             pltpu.VMEM((272, 256), f32),
             pltpu.VMEM((272, 256), f32),
             pltpu.VMEM((3, 16, 256), f32),
-            pltpu.VMEM((128, 256), f32),
             pltpu.VMEM((GROUP, 1024), bf16),
-            pltpu.VMEM((GROUP, 128), f32),
+            pltpu.VMEM((GROUP, 1024), bf16),
         ],
         compiler_params=limits(48),
         name="render",
-    )(tile_ids, counts, active, received, lists, target)
+    )(tile_ids, counts, *segments, received, lists, target)
 
 
 def run_return(camera, gaussians, index, back):
@@ -672,7 +685,8 @@
     lists = tile_lists.reshape(128, 128)
     packed = run_project(camera, gaussians)
     index, send = run_fetch(parity, packed, asked)
-    image, back = run_render(tile_ids, tile_counts, tile_active, send_on(send), lists, target)
+    segments = run_plan(tile_counts, tile_active, index)
+    image, back = run_render(tile_ids, tile_counts, segments, send_on(send), lists, target)
     grads = run_return(camera, gaussians, index, send_on(back))
     return (image, grads)
 

time: 122 us -> 97.9 us (0.80)
  Pallas kernels: 62.4 us -> 38.8 us
  waiting for transfers between devices: 18.1 us -> 14.8 us
  local copies, waits for them, and re-layouts: 3.75 us -> 6.47 us
    pallas_call x1, Pallas kernels: 47.8 us -> 23.2 us  [run_render(): pl.pallas_call(render_kernel, out_shape=(jax.ShapeDtypeStruct((3, 16, 256...]
    all_to_all x2, waiting for transfers between devices: 18.1 us -> 14.8 us  [exchange(): lax.all_to_all(rows.reshape(128, 1, count), AXES, split_axis=0, concat_ax...]
    pallas_call x0 -> x1, Pallas kernels: none -> 3.3 us  [run_plan(): pl.pallas_call(plan_kernel, out_shape=(segments, segments, jax.ShapeDtype...]
    unnamed x18 -> x24, local copies, waits for them, and re-layouts: 2.27 us -> 4.99 us
    pallas_call x1, Pallas kernels: 6.59 us -> 4.35 us  [run_fetch(): pl.pallas_call(fetch_kernel, out_shape=(jax.ShapeDtypeStruct((64, 128), j...]
  transfers between devices with their start and end apart: 2 -> 2, of which waited for: 2 -> 2; matrix products, arithmetic and copies ran while one was open for 0% -> 0% of each run, Pallas kernels for 1% -> 5%
where the time goes in v2:
time: 97.9 us; the launch traced here: 97.5 us
  Pallas kernels  38.8 us (40%)
  blocking collectives  21.1 us (22%)
  starting transfers between devices  15.6 us (16%)
  waiting for transfers between devices  14.8 us (15%)
  local copies, waits for them, and re-layouts  6.47 us (7%)
    pallas_call x1, Pallas kernels, run_render(): pl.pallas_call(render_kernel, out_shape=(jax.ShapeDtypeStruct((3, 16, 256...  23.2 us
    all_to_all x1, blocking collectives, exchange(): lax.all_to_all(rows.reshape(128, 1, count), AXES, split_axis=0, concat_ax...  21.1 us
    all_to_all x2, starting transfers between devices, exchange(): lax.all_to_all(rows.reshape(128, 1, count), AXES, split_axis=0, concat_ax...  15.6 us
    all_to_all x2, waiting for transfers between devices, exchange(): lax.all_to_all(rows.reshape(128, 1, count), AXES, split_axis=0, concat_ax...  14.8 us
    pallas_call x1, Pallas kernels, run_return(): pl.pallas_call(return_kernel, out_shape=jax.ShapeDtypeStruct((59, 8192),...  6.63 us
    unnamed x24, local copies, waits for them, and re-layouts  4.99 us
    pallas_call x1, Pallas kernels, run_fetch(): pl.pallas_call(fetch_kernel, out_shape=(jax.ShapeDtypeStruct((64, 128), j...  4.35 us
    pallas_call x1, Pallas kernels, run_plan(): pl.pallas_call(plan_kernel, out_shape=(segments, segments, jax.ShapeDtype...  3.3 us
  transfers between devices with their start and end apart: 2, of which 2 were waited for; matrix products, arithmetic and copies ran while one was open for 0% of the time, Pallas kernels for 5%

profile of v2, /device:TPU:1, one launch (start us, length us, event | category | flops | bytes accessed | tf_op | source)
XLA Modules:
  0.0 97.5 jit_solution(2743903792750338445)
XLA Ops:
  0.6 0.0 copy-start.11
  0.6 0.0 copy-start.5
  0.7 0.0 copy-start.4
  0.7 0.0 copy-start.10
  0.7 1.5 %broadcast_in_dim.3 = s32[64,2,128]{2,1,0:T(2,128)} broadcast(s32[64,128]{1,0:T(8,128)} %bitcast.12), dimensions={0,2} | broadcast | bytes 98304 | tf_op jit(solution)/shard_map/broadcast_in_dim | solution.py:695
  2.1 11.5 %all-to-all-start = ((s32[128,1,128]{2,1,0:T(1,128)}), s32[128,1,128]{2,1,0:T(1,128)S(1)}, u32[]{:S(2)}, u32[]{:S(2)}) async-start(s32[128,1,128]{2,1,0:T(1,128)} %bitcast.2), calls=%async_computation | async-start | bytes 131072 | tf_op jit(solution)/shard_map/all_to_all | solution.py:680
  13.6 0.0 copy-start
  13.7 1.6 %copy-done = f32[59,8192]{1,0:T(8,128)S(1)} copy-done((f32[59,8192]{1,0:T(8,128)S(1)}, f32[59,8192]{1,0:T(8,128)}, u32[]{:S(2)}) %copy-start) | copy-done | bytes 1933336
  15.2 0.0 copy-start.6
  15.2 0.7 copy-done.6
  15.9 0.0 copy-start.1
  15.9 0.0 copy-start.7
  15.9 1.4 %project.1.packed_ref = bf16[640,256]{1,0:T(8,128)(2,1)S(1)} custom-call(f32[4]{0:T(128)S(1)} %copy-done.6, f32[59,8192]{1,0:T(8,128)S(1)} %copy-done), custom_call_target="tpu_custom_call" | custom-call | tf_op jit(solution)/shard_map/project/pallas_call | solution.py:586
  17.3 6.1 %all-to-all-done = s32[128,1,128]{2,1,0:T(1,128)S(1)} async-done(((s32[128,1,128]{2,1,0:T(1,128)}), s32[128,1,128]{2,1,0:T(1,128)S(1)}, u32[]{:S(2)}, u32[]{:S(2)}) %all-to-all-start) | async-done | bytes 65568 | tf_op jit(solution)/shard_map/all_to_all | solution.py:680
  23.4 4.4 %fetch.1 = (s32[64,128]{1,0:T(8,128)S(1)}, f32[640,128]{1,0:T(8,128)}) custom-call(s32[1]{0:T(128)} %bitcast.parity_ref, bf16[640,256]{1,0:T(8,128)(2,1)S(1)} %project.1.packed_ref, s32[128,128]{1,0:T(8,128)S(1)} %bitcast.11), custom_call_target="tpu_custom_call" | custom-call | tf_op jit(solution)/shard_map/fetch/pallas_call | solution.py:598
  27.8 0.0 copy-start.2
  27.8 0.6 copy-done.2
  28.4 4.1 %all-to-all-start.1 = ((f32[128,1,640]{2,1,0:T(1,128)}), f32[128,1,640]{2,1,0:T(1,128)S(1)}, u32[]{:S(2)}, u32[]{:S(2)}) async-start(f32[128,1,640]{2,1,0:T(1,128)} %bitcast.4), calls=%async_computation.1 | async-start | bytes 655360 | tf_op jit(solution)/shard_map/all_to_all | solution.py:680
  32.5 0.0 copy-done.11
  32.5 3.3 %plan.1 = (s32[160]{0:T(256)}, s32[160]{0:T(256)}, s32[1]{0:T(128)}) custom-call(s32[1,16]{1,0:T(1,128)} %counts_ref.3, s32[1,16]{1,0:T(1,128)} %active_ref.1, s32[64,128]{1,0:T(8,128)} %copy-done.2), custom_call_target="tpu_custom_call" | custom-call | tf_op jit(solution)/shard_map/plan/pallas_call | solution.py:614
  35.8 8.7 %all-to-all-done.1 = f32[128,1,640]{2,1,0:T(1,128)S(1)} async-done(((f32[128,1,640]{2,1,0:T(1,128)}), f32[128,1,640]{2,1,0:T(1,128)S(1)}, u32[]{:S(2)}, u32[]{:S(2)}) %all-to-all-start.1) | async-done | bytes 327712 | tf_op jit(solution)/shard_map/all_to_all | solution.py:680
  44.5 0.0 copy-done.5
  44.5 0.0 copy-done.4
  44.5 0.0 copy-done.10
  44.5 0.0 copy-start.8
  44.5 0.7 copy-done.8
  45.2 0.0 copy-start.9
  45.2 0.7 copy-done.9
  45.9 23.2 %render.1 = (f32[3,16,256]{2,1,0:T(8,128)}, f32[640,128]{1,0:T(8,128)S(1)}) custom-call(s32[1,16]{1,0:T(1,128)S(1)} %copy-done.10, s32[1,16]{1,0:T(1,128)S(1)} %copy-done.5, s32[160]{0:T(256)S(1)} %copy-done.8, s32[160]{0:T(256)S(1)} %copy-done.9, s32[1]{0:T(128)} %get-tuple-element.12.groups_ref, f32[640,128]{1,0:T(8,128)S(1)} %bitcast.9, ...), custom_call_target="tpu_custom_call" | custom-call | tf_op jit(solution)/shard_map/render/pallas_call | solution.py:626
  69.0 21.1 %all_to_all.15 = f32[128,1,640]{2,1,0:T(1,128)S(1)} all-to-all(f32[128,1,640]{2,1,0:T(1,128)S(1)} %bitcast.10), channel_id=1, replica_groups=mesh['tile'=32,'shard'=4] {'tile','shard'}, dimensions={0} | all-to-all | bytes 655360 | tf_op jit(solution)/shard_map/all_to_all | solution.py:680
  90.1 0.0 copy-done.1
  90.1 0.0 copy-done.7
  90.1 0.0 copy-start.3
  90.1 0.8 copy-done.3
  90.9 6.6 %give_back.1 = f32[59,8192]{1,0:T(8,128)} custom-call(f32[4]{0:T(128)S(1)} %copy-done.7, f32[59,8192]{1,0:T(8,128)S(1)} %copy-done.1, s32[64,128]{1,0:T(8,128)S(1)} %copy-done.3, f32[640,128]{1,0:T(8,128)S(1)} %bitcast.8), custom_call_target="tpu_custom_call" | custom-call | tf_op jit(solution)/shard_map/give_back/pallas_call | solution.py:663
  (1 shorter events, 0.0 us)
Async XLA Ops:
  0.6 31.9 %copy-start.11 = (s32[1,16,1024]{2,1,0:T(8,128)S(1)}, s32[1,16,1024]{2,1,0:T(8,128)}, u32[]{:S(2)}) copy-start(s32[1,16,1024]{2,1,0:T(8,128)} %param.12) | copy-start | bytes 196612
  0.6 43.9 %copy-start.5 = (s32[1,16]{1,0:T(1,128)S(1)}, s32[1,16]{1,0:T(1,128)}, u32[]{:S(2)}) copy-start(s32[1,16]{1,0:T(1,128)} %counts_ref.3) | copy-start | bytes 196
  0.7 43.9 %copy-start.4 = (f32[3,16,256]{2,1,0:T(8,128)S(1)}, f32[3,16,256]{2,1,0:T(8,128)}, u32[]{:S(2)}) copy-start(f32[3,16,256]{2,1,0:T(8,128)} %target_ref.1) | copy-start | bytes 147460
  0.7 43.9 %copy-start.10 = (s32[1,16]{1,0:T(1,128)S(1)}, s32[1,16]{1,0:T(1,128)}, u32[]{:S(2)}) copy-start(s32[1,16]{1,0:T(1,128)} %ids_ref.1) | copy-start | bytes 196
  2.1 21.3 %all-to-all-start = ((s32[128,1,128]{2,1,0:T(1,128)}), s32[128,1,128]{2,1,0:T(1,128)S(1)}, u32[]{:S(2)}, u32[]{:S(2)}) async-start(s32[128,1,128]{2,1,0:T(1,128)} %bitcast.2), calls=%async_computation | async-start | bytes 131072 | tf_op jit(solution)/shard_map/all_to_all | solution.py:680
  13.6 1.6 %copy-start = (f32[59,8192]{1,0:T(8,128)S(1)}, f32[59,8192]{1,0:T(8,128)}, u32[]{:S(2)}) copy-start(f32[59,8192]{1,0:T(8,128)} %gaussians_ref.3) | copy-start | bytes 5799940
  15.2 0.7 copy-start.6
  15.9 74.2 %copy-start.1 = (f32[59,8192]{1,0:T(8,128)S(1)}, f32[59,8192]{1,0:T(8,128)}, u32[]{:S(2)}) copy-start(f32[59,8192]{1,0:T(8,128)} %gaussians_ref.3) | copy-start | bytes 5799940
  15.9 74.2 %copy-start.7 = (f32[4]{0:T(128)S(1)}, f32[4]{0:T(128)}, u32[]{:S(2)}) copy-start(f32[4]{0:T(128)} %camera_ref.3) | copy-start | bytes 52
  27.8 0.6 copy-start.2
  28.4 16.1 %all-to-all-start.1 = ((f32[128,1,640]{2,1,0:T(1,128)}), f32[128,1,640]{2,1,0:T(1,128)S(1)}, u32[]{:S(2)}, u32[]{:S(2)}) async-start(f32[128,1,640]{2,1,0:T(1,128)} %bitcast.4), calls=%async_computation.1 | async-start | bytes 655360 | tf_op jit(solution)/shard_map/all_to_all | solution.py:680
  44.5 0.7 copy-start.8
  45.2 0.7 copy-start.9
  90.1 0.8 copy-start.3

commit v3 on v2

--- a/solution.py
+++ b/solution.py
@@ -253,7 +253,28 @@
     pack_table(table_ref, packed_ref)
 
 
-def fetch_kernel(parity_ref, packed_ref, asked_ref, index_ref, send_ref, table_ref):
+def plan_segments(counts_ref, active_ref):
+    slot = lax.broadcasted_iota(jnp.int32, (1, 256), 1)
+    end = jnp.int32(0)
+    tile = jnp.zeros((1, 256), jnp.int32)
+    first = jnp.zeros((1, 256), jnp.int32)
+    for t in range(16):
+        used = jnp.where(active_ref[0, t] > 0, (counts_ref[0, t] + (SEG - 1)) >> 6, 0)
+        end = end + used
+        past = slot >= end
+        tile = tile + jnp.where(past, 1, 0)
+        first = first + jnp.where(past, used, 0)
+    spare = slot >= end
+    tile = jnp.where(spare, 0, tile)
+    place = jnp.where(spare, 16, slot - first)
+    groups = jnp.zeros((1, 256), jnp.int32) + ((end + (SEGS - 1)) >> 4)
+    return jnp.concatenate([tile, place, groups, groups], axis=0)
+
+
+def fetch_kernel(
+    parity_ref, counts_ref, active_ref, packed_ref, asked_ref, index_ref, send_ref, plan_ref, table_ref
+):
+    plan_ref[...] = plan_segments(counts_ref, active_ref)
     low = low_half((64, 128))
     even = asked_ref[pl.ds(0, 64, stride=2), :]
     odd = asked_ref[pl.ds(1, 64, stride=2), :]
@@ -313,34 +334,10 @@
     return [jnp.ones((1, 256), jnp.float32), x, y, x * x, x * y, y * y]
 
 
-def plan_kernel(counts_ref, active_ref, after_ref, seg_tile, seg_place, groups_ref):
-    def clear(n, carry):
-        seg_tile[n] = 0
-        seg_place[n] = 16
-        return carry
-
-    lax.fori_loop(0, SEGS * (MAX_GROUPS + 1), clear, 0)
-
-    def add_tile(t, n):
-        used = jnp.where(active_ref[0, t] > 0, (counts_ref[0, t] + (SEG - 1)) >> 6, 0)
-
-        def add_segment(k, m):
-            seg_tile[m] = t
-            seg_place[m] = k
-            return m + 1
-
-        return lax.fori_loop(0, used, add_segment, n)
-
-    segments = lax.fori_loop(0, 16, add_tile, 0)
-    groups_ref[0] = (segments + (SEGS - 1)) // SEGS
-
-
 def render_kernel(
     ids_ref,
     counts_ref,
-    seg_tile,
-    seg_place,
-    groups_ref,
+    plan_ref,
     recv_ref,
     lists_ref,
     target_ref,
@@ -368,7 +365,7 @@
     pieces_a_ref,
     pieces_b_ref,
 ):
-    groups = groups_ref[0]
+    groups = plan_ref[2, 0]
     blocks_to_table(recv_ref, table_ref)
     pack_table(table_ref, packed_ref)
     total_ref[...] = jnp.zeros_like(total_ref)
@@ -392,7 +389,7 @@
             pair = []
             for half in range(2):
                 n = SEGS * g + 2 * c + half
-                t, place = seg_tile[n], seg_place[n]
+                t, place = plan_ref[0, n], plan_ref[1, n]
                 near = jnp.minimum(place, 15)
                 row = lists_ref[pl.ds(t * 8 + (near >> 1), 1), :]
                 row = jnp.where((near & 1) == half, row, swap(row))
@@ -455,7 +452,7 @@
             lights = [lights[k] + weight * tint[:, 18 + k : 19 + k] for k in range(3)]
         for s in range(SEGS):
             n = SEGS * g + s
-            spot = seg_place[n] * 16 + seg_tile[n]
+            spot = plan_ref[1, n] * 16 + plan_ref[0, n]
             pass_ref[pl.ds(spot, 1), :] = transmit[s : s + 1]
             for k in range(3):
                 light_ref[k, pl.ds(spot, 1), :] = lights[k][s : s + 1]
@@ -503,8 +500,8 @@
 
     def backward(g, pieces_ref):
         first = pl.multiple_of(g * GROUP, GROUP)
-        tiles = [seg_tile[SEGS * g + s] for s in range(SEGS)]
-        spots = [seg_place[SEGS * g + s] * 16 + tiles[s] for s in range(SEGS)]
+        tiles = [plan_ref[0, SEGS * g + s] for s in range(SEGS)]
+        spots = [plan_ref[1, SEGS * g + s] * 16 + tiles[s] for s in range(SEGS)]
         start = rows_at(start_ref, spots)
         behind = rows_at(behind_ref, spots)
         resid = [rows_at(resid_ref.at[k], tiles) for k in range(3)]
@@ -527,7 +524,7 @@
         first = pl.multiple_of(g * GROUP, GROUP)
         wide = wide_ref[pl.ds(first, GROUP), :]
         known = jnp.concatenate([wide[128 * c : 128 * c + 128].T for c in range(GROUP // 128)], axis=1)
-        tiles = [seg_tile[SEGS * g + s] for s in range(SEGS)]
+        tiles = [plan_ref[0, SEGS * g + s] for s in range(SEGS)]
         resid = [parts(rows_at(resid_ref.at[k], tiles), 2) for k in range(3)]
         resid = jnp.concatenate([resid[k][step] for step in range(2) for k in range(3)], axis=0)
         moments = across(moment_ref[...], pieces_ref[:, 0:512])
@@ -594,33 +591,23 @@
     )(camera, gaussians)
 
 
-def run_fetch(parity, packed, asked):
+def run_fetch(parity, counts, active, packed, asked):
     return pl.pallas_call(
         fetch_kernel,
         out_shape=(
             jax.ShapeDtypeStruct((64, 128), jnp.int32),
             jax.ShapeDtypeStruct((640, 128), jnp.float32),
+            jax.ShapeDtypeStruct((4, 256), jnp.int32),
         ),
-        in_specs=[smem(), vmem(), vmem()],
-        out_specs=(vmem(), vmem()),
+        in_specs=[smem(), smem(), smem(), vmem(), vmem()],
+        out_specs=(vmem(), vmem(), vmem()),
         scratch_shapes=[pltpu.VMEM((FEATS, 64, 128), jnp.float32)],
         compiler_params=limits(16),
         name="fetch",
-    )(parity, packed, asked)
-
-
-def run_plan(counts, active, after):
-    segments = jax.ShapeDtypeStruct((SEGS * (MAX_GROUPS + 1),), jnp.int32)
-    return pl.pallas_call(
-        plan_kernel,
-        out_shape=(segments, segments, jax.ShapeDtypeStruct((1,), jnp.int32)),
-        in_specs=[smem(), smem(), pl.BlockSpec(memory_space=pl.ANY)],
-        out_specs=(smem(), smem(), smem()),
-        name="plan",
-    )(counts, active, after)
-
-
-def run_render(tile_ids, counts, segments, received, lists, target):
+    )(parity, counts, active, packed, asked)
+
+
+def run_render(tile_ids, counts, plan, received, lists, target):
     f32, bf16 = jnp.float32, jnp.bfloat16
     entries = (MAX_GROUPS + 1) * GROUP
     return pl.pallas_call(
@@ -629,7 +616,7 @@
             jax.ShapeDtypeStruct((3, 16, 256), f32),
             jax.ShapeDtypeStruct((640, 128), f32),
         ),
-        in_specs=[smem()] * 5 + [vmem()] * 3,
+        in_specs=[smem()] * 3 + [vmem()] * 3,
         out_specs=(vmem(), vmem()),
         scratch_shapes=[
             pltpu.VMEM((FEATS, 64, 128), f32),
@@ -656,7 +643,7 @@
         ],
         compiler_params=limits(48),
         name="render",
-    )(tile_ids, counts, *segments, received, lists, target)
+    )(tile_ids, counts, plan, received, lists, target)
 
 
 def run_return(camera, gaussians, index, back):
@@ -684,9 +671,8 @@
 def local(gaussians, camera, asked, parity, tile_ids, tile_lists, tile_counts, tile_active, target, send_on):
     lists = tile_lists.reshape(128, 128)
     packed = run_project(camera, gaussians)
-    index, send = run_fetch(parity, packed, asked)
-    segments = run_plan(tile_counts, tile_active, index)
-    image, back = run_render(tile_ids, tile_counts, segments, send_on(send), lists, target)
+    index, send, plan = run_fetch(parity, tile_counts, tile_active, packed, asked)
+    image, back = run_render(tile_ids, tile_counts, plan, send_on(send), lists, target)
     grads = run_return(camera, gaussians, index, send_on(back))
     return (image, grads)
 

time: 97.9 us -> 95 us (0.970)
  Pallas kernels: 38.8 us -> 29.9 us
  blocking collectives: 21.1 us -> 26.7 us
  waiting for transfers between devices: 14.8 us -> 18.1 us
  local copies, waits for them, and re-layouts: 6.47 us -> 3.75 us
    pallas_call x1, Pallas kernels: 23.2 us -> 16.9 us  [run_render(): pl.pallas_call(render_kernel, out_shape=(jax.ShapeDtypeStruct((3, 16, 256...]
    all_to_all x1, blocking collectives: 21.1 us -> 26.7 us  [exchange(): lax.all_to_all(rows.reshape(128, 1, count), AXES, split_axis=0, concat_ax...]
    all_to_all x2, waiting for transfers between devices: 14.8 us -> 18.1 us  [exchange(): lax.all_to_all(rows.reshape(128, 1, count), AXES, split_axis=0, concat_ax...]
    pallas_call x1 -> x0, Pallas kernels: 3.3 us -> none  [run_plan(): pl.pallas_call(plan_kernel, out_shape=(segments, segments, jax.ShapeDtype...]
    unnamed x24 -> x18, local copies, waits for them, and re-layouts: 4.99 us -> 2.27 us
  transfers between devices with their start and end apart: 2 -> 2, of which waited for: 2 -> 2; matrix products, arithmetic and copies ran while one was open for 0% -> 0% of each run, Pallas kernels for 5% -> 1%
where the time goes in v3:
time: 95 us; the launch traced here: 94.7 us
  Pallas kernels  29.9 us (31%)
  blocking collectives  26.7 us (28%)
  waiting for transfers between devices  18.1 us (19%)
  starting transfers between devices  15.6 us (16%)
  local copies, waits for them, and re-layouts  3.75 us (4%)
    all_to_all x1, blocking collectives, exchange(): lax.all_to_all(rows.reshape(128, 1, count), AXES, split_axis=0, concat_ax...  26.7 us
    all_to_all x2, waiting for transfers between devices, exchange(): lax.all_to_all(rows.reshape(128, 1, count), AXES, split_axis=0, concat_ax...  18.1 us
    pallas_call x1, Pallas kernels, run_render(): pl.pallas_call(render_kernel, out_shape=(jax.ShapeDtypeStruct((3, 16, 256...  16.9 us
    all_to_all x2, starting transfers between devices, exchange(): lax.all_to_all(rows.reshape(128, 1, count), AXES, split_axis=0, concat_ax...  15.6 us
    pallas_call x1, Pallas kernels, run_return(): pl.pallas_call(return_kernel, out_shape=jax.ShapeDtypeStruct((59, 8192),...  6.63 us
    pallas_call x1, Pallas kernels, run_fetch(): pl.pallas_call(fetch_kernel, out_shape=(jax.ShapeDtypeStruct((64, 128), j...  4.89 us
    unnamed x18, local copies, waits for them, and re-layouts  2.27 us
  transfers between devices with their start and end apart: 2, of which 2 were waited for; matrix products, arithmetic and copies ran while one was open for 0% of the time, Pallas kernels for 1%

profile of v3, /device:TPU:1, one launch (start us, length us, event | category | flops | bytes accessed | tf_op | source)
XLA Modules:
  0.0 94.7 jit_solution(9333021356934127683)
XLA Ops:
  0.6 0.0 copy-start.3
  0.6 0.0 copy-start.6
  0.7 0.0 copy-start.8
  0.7 0.0 copy-start.2
  0.7 0.0 copy-start.7
  0.7 1.5 %broadcast_in_dim.3 = s32[64,2,128]{2,1,0:T(2,128)} broadcast(s32[64,128]{1,0:T(8,128)} %bitcast.12), dimensions={0,2} | broadcast | bytes 98304 | tf_op jit(solution)/shard_map/broadcast_in_dim | solution.py:681
  2.1 11.5 %all-to-all-start = ((s32[128,1,128]{2,1,0:T(1,128)}), s32[128,1,128]{2,1,0:T(1,128)S(1)}, u32[]{:S(2)}, u32[]{:S(2)}) async-start(s32[128,1,128]{2,1,0:T(1,128)} %bitcast.2), calls=%async_computation | async-start | bytes 131072 | tf_op jit(solution)/shard_map/all_to_all | solution.py:667
  13.7 0.0 copy-start
  13.7 1.6 %copy-done = f32[59,8192]{1,0:T(8,128)S(1)} copy-done((f32[59,8192]{1,0:T(8,128)S(1)}, f32[59,8192]{1,0:T(8,128)}, u32[]{:S(2)}) %copy-start) | copy-done | bytes 1933336
  15.3 0.0 copy-start.4
  15.3 0.7 copy-done.4
  15.9 0.0 copy-start.1
  15.9 0.0 copy-start.5
  15.9 1.4 %project.1.packed_ref = bf16[640,256]{1,0:T(8,128)(2,1)S(1)} custom-call(f32[4]{0:T(128)S(1)} %copy-done.4, f32[59,8192]{1,0:T(8,128)S(1)} %copy-done), custom_call_target="tpu_custom_call" | custom-call | tf_op jit(solution)/shard_map/project/pallas_call | solution.py:583
  17.3 6.1 %all-to-all-done = s32[128,1,128]{2,1,0:T(1,128)S(1)} async-done(((s32[128,1,128]{2,1,0:T(1,128)}), s32[128,1,128]{2,1,0:T(1,128)S(1)}, u32[]{:S(2)}, u32[]{:S(2)}) %all-to-all-start) | async-done | bytes 65568 | tf_op jit(solution)/shard_map/all_to_all | solution.py:667
  23.5 0.0 copy-done.3
  23.5 0.0 copy-done.6
  23.5 4.9 %fetch.1 = (s32[64,128]{1,0:T(8,128)S(1)}, f32[640,128]{1,0:T(8,128)}, s32[4,256]{1,0:T(4,128)S(1)}) custom-call(s32[1]{0:T(128)} %bitcast.parity_ref, s32[1,16]{1,0:T(1,128)S(1)} %copy-done.3, s32[1,16]{1,0:T(1,128)S(1)} %copy-done.6, bf16[640,256]{1,0:T(8,128)(2,1)S(1)} %project.1.packed_ref, s32[128,128]{1,0:T(8,128)S(1)} %bitcast.11), custom_call_target="tpu_custom_call" | custom-call | tf_op jit(solution)/shard_map/fetch/pallas_call | solution.py:595
  28.4 4.1 %all-to-all-start.1 = ((f32[128,1,640]{2,1,0:T(1,128)}), f32[128,1,640]{2,1,0:T(1,128)S(1)}, u32[]{:S(2)}, u32[]{:S(2)}) async-start(f32[128,1,640]{2,1,0:T(1,128)} %bitcast.4), calls=%async_computation.1 | async-start | bytes 655360 | tf_op jit(solution)/shard_map/all_to_all | solution.py:667
  32.4 0.0 copy-done.8
  32.5 12.0 %all-to-all-done.1 = f32[128,1,640]{2,1,0:T(1,128)S(1)} async-done(((f32[128,1,640]{2,1,0:T(1,128)}), f32[128,1,640]{2,1,0:T(1,128)S(1)}, u32[]{:S(2)}, u32[]{:S(2)}) %all-to-all-start.1) | async-done | bytes 327712 | tf_op jit(solution)/shard_map/all_to_all | solution.py:667
  44.5 0.0 copy-done.2
  44.5 0.0 copy-done.7
  44.5 16.9 %render.1 = (f32[3,16,256]{2,1,0:T(8,128)}, f32[640,128]{1,0:T(8,128)S(1)}) custom-call(s32[1,16]{1,0:T(1,128)S(1)} %copy-done.7, s32[1,16]{1,0:T(1,128)S(1)} %copy-done.3, s32[4,256]{1,0:T(4,128)S(1)} %get-tuple-element.7.plan_ref, f32[640,128]{1,0:T(8,128)S(1)} %bitcast.9, s32[128,128]{1,0:T(8,128)S(1)} %reshape.33.lists_ref, f32[3,16,256]{2,1,0:T(8,128)S(1)} %copy-done.2), custom_call_target="tpu_custom_call" | custom-call | tf_op jit(solution)/shard_map/render/pallas_call | solution.py:613
  61.4 26.7 %all_to_all.15 = f32[128,1,640]{2,1,0:T(1,128)S(1)} all-to-all(f32[128,1,640]{2,1,0:T(1,128)S(1)} %bitcast.10), channel_id=1, replica_groups=mesh['tile'=32,'shard'=4] {'tile','shard'}, dimensions={0} | all-to-all | bytes 655360 | tf_op jit(solution)/shard_map/all_to_all | solution.py:667
  88.1 0.0 copy-done.1
  88.1 0.0 copy-done.5
  88.1 6.6 %give_back.1 = f32[59,8192]{1,0:T(8,128)} custom-call(f32[4]{0:T(128)S(1)} %copy-done.5, f32[59,8192]{1,0:T(8,128)S(1)} %copy-done.1, s32[64,128]{1,0:T(8,128)S(1)} %get-tuple-element.10.index_ref, f32[640,128]{1,0:T(8,128)S(1)} %bitcast.8), custom_call_target="tpu_custom_call" | custom-call | tf_op jit(solution)/shard_map/give_back/pallas_call | solution.py:650
  (1 shorter events, 0.0 us)
Async XLA Ops:
  0.6 22.8 %copy-start.3 = (s32[1,16]{1,0:T(1,128)S(1)}, s32[1,16]{1,0:T(1,128)}, u32[]{:S(2)}) copy-start(s32[1,16]{1,0:T(1,128)} %counts_ref.3) | copy-start | bytes 196
  0.6 22.8 %copy-start.6 = (s32[1,16]{1,0:T(1,128)S(1)}, s32[1,16]{1,0:T(1,128)}, u32[]{:S(2)}) copy-start(s32[1,16]{1,0:T(1,128)} %active_ref.1) | copy-start | bytes 196
  0.7 31.8 %copy-start.8 = (s32[1,16,1024]{2,1,0:T(8,128)S(1)}, s32[1,16,1024]{2,1,0:T(8,128)}, u32[]{:S(2)}) copy-start(s32[1,16,1024]{2,1,0:T(8,128)} %param.12) | copy-start | bytes 196612
  0.7 43.8 %copy-start.2 = (f32[3,16,256]{2,1,0:T(8,128)S(1)}, f32[3,16,256]{2,1,0:T(8,128)}, u32[]{:S(2)}) copy-start(f32[3,16,256]{2,1,0:T(8,128)} %target_ref.1) | copy-start | bytes 147460
  0.7 43.8 %copy-start.7 = (s32[1,16]{1,0:T(1,128)S(1)}, s32[1,16]{1,0:T(1,128)}, u32[]{:S(2)}) copy-start(s32[1,16]{1,0:T(1,128)} %ids_ref.1) | copy-start | bytes 196
  2.1 21.3 %all-to-all-start = ((s32[128,1,128]{2,1,0:T(1,128)}), s32[128,1,128]{2,1,0:T(1,128)S(1)}, u32[]{:S(2)}, u32[]{:S(2)}) async-start(s32[128,1,128]{2,1,0:T(1,128)} %bitcast.2), calls=%async_computation | async-start | bytes 131072 | tf_op jit(solution)/shard_map/all_to_all | solution.py:667
  13.7 1.6 %copy-start = (f32[59,8192]{1,0:T(8,128)S(1)}, f32[59,8192]{1,0:T(8,128)}, u32[]{:S(2)}) copy-start(f32[59,8192]{1,0:T(8,128)} %gaussians_ref.3) | copy-start | bytes 5799940
  15.3 0.7 copy-start.4
  15.9 72.2 %copy-start.1 = (f32[59,8192]{1,0:T(8,128)S(1)}, f32[59,8192]{1,0:T(8,128)}, u32[]{:S(2)}) copy-start(f32[59,8192]{1,0:T(8,128)} %gaussians_ref.3) | copy-start | bytes 5799940
  15.9 72.2 %copy-start.5 = (f32[4]{0:T(128)S(1)}, f32[4]{0:T(128)}, u32[]{:S(2)}) copy-start(f32[4]{0:T(128)} %camera_ref.3) | copy-start | bytes 52
  28.4 16.1 %all-to-all-start.1 = ((f32[128,1,640]{2,1,0:T(1,128)}), f32[128,1,640]{2,1,0:T(1,128)S(1)}, u32[]{:S(2)}, u32[]{:S(2)}) async-start(f32[128,1,640]{2,1,0:T(1,128)} %bitcast.4), calls=%async_computation.1 | async-start | bytes 655360 | tf_op jit(solution)/shard_map/all_to_all | solution.py:667
